TPU v7x, 128 devices: a whole 4x4x4 slice. The times are simulated.
128 devices in a mesh: grp: 4 (over z), env: 32 (over x, y, core).
Axes of the slice: x: 4, y: 4, z: 4, core: 2. Of those that a mesh axis runs over, the one named last changes fastest.
Arguments:
- images: bfloat16 [256, 4, 36, 768], P(('grp', 'env')), may hold values from -6 to 6
- camera_counts: int32 [256], P(('grp', 'env')), may hold values from 1 to 4, as said below
- slot_of: int32 [256], replicated, may hold values from 0 to 255, each once
- patch_weight: bfloat16 [768, 384], replicated, may hold values from -0.21875 to 0.21875
- pos_embed: bfloat16 [36, 384], replicated, may hold values from -3 to 3
- attn_gain: float32 [2, 384], replicated, may hold values from 0.25 to 1.75
- qkv_weight: bfloat16 [2, 384, 1152], replicated, may hold values from -0.3125 to 0.3125
- proj_weight: bfloat16 [2, 384, 384], replicated, may hold values from -0.3125 to 0.3125
- mlp_gain: float32 [2, 384], replicated, may hold values from 0.25 to 1.75
- up_weight: bfloat16 [2, 384, 1536], replicated, may hold values from -0.3125 to 0.3125
- down_weight: bfloat16 [2, 1536, 384], replicated, may hold values from -0.15625 to 0.15625
- final_gain: float32 [384], replicated, may hold values from 0.25 to 1.75
- cotangent: bfloat16 [256, 384], P(('grp', 'env')), may hold values from -6 to 6
Outputs:
- learner_tokens: bfloat16 [256, 384], P(('grp', 'env'))
- grad_patch: float32 [768, 384], P(('grp', 'env'))
- grad_qkv: float32 [2, 384, 1152], P(None, ('grp', 'env'))
- grad_proj: float32 [2, 384, 384], P(None, ('grp', 'env'))
- grad_up: float32 [2, 384, 1536], P(None, ('grp', 'env'))
- grad_down: float32 [2, 1536, 384], P(None, ('grp', 'env'))
Inputs may be any that keep to these rules, and one draw needn't show every extreme that they name: `camera_counts`: split the environments into aligned blocks of 2. No block holds more than 7 cameras, and blocks b and b + 16 within the same run of 32 blocks (runs aligned) hold together at most 10 cameras; in every run both bounds are reached.
All inputs are finite; a program needn't handle non-finite values.
Results may differ from a plain program's by a relative error of at most 0.018.
Values may be sent and summed in bfloat16 or wider, within the bound.
No kernel may reach another device: no remote copies, remote signals or barrier semaphores. Data moves between devices by JAX's collectives and lax.ppermute only.
A program may use at most 128 MiB of HBM per device.

v0:
```python
from functools import partial

import jax
import jax.numpy as jnp
from jax import lax
from jax.experimental import pallas as pl
from jax.experimental.pallas import tpu as pltpu
from jax.sharding import PartitionSpec as P

F32 = jnp.float32
BF16 = jnp.bfloat16
D = 384
FF = 1536
WIDE = 768
HEADS = 6
PATCHES = 36
PATCH_DIM = 768
CAMS = 4
SLOTS = 8
CAM_MOST = 7
ROWS = 256
VMEM_BYTES = 20 * 1024 * 1024
SMALL_VMEM_BYTES = 14 * 1024 * 1024
EPS = 1e-06


def mm(left, right):
    return jnp.dot(left, right, preferred_element_type=F32)


def mm_nt(left, right):
    return lax.dot_general(left, right, (((1,), (1,)), ((), ())), preferred_element_type=F32)


def mm_tn(left, right):
    return lax.dot_general(left, right, (((0,), (0,)), ((), ())), preferred_element_type=F32)


def exact_mm(left, right):
    return jnp.dot(left, right, preferred_element_type=F32, precision=lax.Precision.HIGHEST)


def iota(shape, dim):
    return lax.broadcasted_iota(jnp.int32, shape, dim)


def steps_of(value, step, count):
    total = jnp.zeros_like(value)
    for at in range(1, count):
        total = total + jnp.where(value >= at * step, 1, 0)
    return total


def norm_rows(values, gain_row):
    centered = values - jnp.mean(values, axis=-1, keepdims=True)
    spread = jnp.mean(centered * centered, axis=-1, keepdims=True)
    return centered * lax.rsqrt(spread + EPS) * gain_row


def norm_pull(values, gain_row, upstream):
    centered = values - jnp.mean(values, axis=-1, keepdims=True)
    inv = lax.rsqrt(jnp.mean(centered * centered, axis=-1, keepdims=True) + EPS)
    hat = centered * inv
    scaled = upstream * gain_row
    return inv * (
        scaled
        - jnp.mean(scaled, axis=-1, keepdims=True)
        - hat * jnp.mean(scaled * hat, axis=-1, keepdims=True)
    )


def gelu_and_slope(before):
    size = jnp.abs(before)
    bell = jnp.exp(before * before * -0.5)
    t = 1.0 / (1.0 + (0.3275911 * 0.7071067811865476) * size)
    poly = t * (
        0.5 * 0.254829592
        + t
        * (
            0.5 * -0.284496736
            + t * (0.5 * 1.421413741 + t * (0.5 * -1.453152027 + t * (0.5 * 1.061405429)))
        )
    )
    tail = poly * bell
    below = jnp.where(before > 0, 1.0 - tail, tail)
    return before * below, below + before * bell * 0.3989422804014327


def camera_bias():
    cam_row = steps_of(iota((ROWS, 1), 0), PATCHES, CAM_MOST + 1)
    cam_col = steps_of(iota((1, ROWS), 1), PATCHES, CAM_MOST + 1)
    return jnp.where(cam_row == cam_col, 0.0, -1e30)


def head_mask(width_lanes, which):
    lane = iota((1, width_lanes), 1)
    return lane < 64 if which == 0 else lane >= 64


def attention_half(stream, gain_a, qkv, proj, store, need):
    normed_s, triple_s, probs_s, mixed_s, middle_s = store
    normed_s[...] = norm_rows(stream, gain_a).astype(BF16)
    need(0)
    triple_s[...] = mm(normed_s[...], qkv[...]).astype(BF16)
    bias = camera_bias()
    for pair in range(3):
        q = triple_s[:, pl.ds(pair * 128, 128)]
        k = triple_s[:, pl.ds(D + pair * 128, 128)]
        v = triple_s[:, pl.ds(2 * D + pair * 128, 128)]
        mixed = None
        for h in range(2):
            mask = head_mask(128, h)
            scores = mm_nt(jnp.where(mask, q * 0.125, 0.0).astype(BF16), k) + bias
            raised = jnp.exp(scores)
            probs = (raised * (1.0 / jnp.sum(raised, axis=-1, keepdims=True))).astype(BF16)
            probs_s[pair * 2 + h] = probs
            part = mm(probs, jnp.where(mask, v, 0.0).astype(BF16))
            mixed = part if mixed is None else mixed + part
        mixed_s[:, pl.ds(pair * 128, 128)] = mixed.astype(BF16)
    need(1)
    middle_s[...] = stream + mm(mixed_s[...], proj[...])


def mlp_half(middle, gain_m, up, down, store):
    second_s, hidden_s, slope_s = store
    second_s[...] = norm_rows(middle, gain_m).astype(BF16)
    total = middle
    for j in range(FF // WIDE):
        cols = pl.ds(j * WIDE, WIDE)
        hidden, slope = gelu_and_slope(mm(second_s[...], up[:, cols]))
        slope_s[:, cols] = slope.astype(BF16)
        hidden_s[:, cols] = hidden.astype(BF16)
        total = total + mm(hidden_s[:, cols], down[cols, :])
    return total


def pick(order, width=D):
    return jnp.where(order == iota((D, width), 1), 1.0, 0.0).astype(BF16)


def own_first(my_core):
    p = iota((D, 1), 0)
    swap = jnp.where(p >= D // 2, 1, 0)
    core = jnp.where(swap == my_core, 0, 1)
    return core, p - swap * (D // 2)


def order_three(my_core):
    core, rest = own_first(my_core)
    first = steps_of(rest, 48, 4)
    rest = rest - first * 48
    r = steps_of(rest, 16, 3)
    rest = rest - r * 16
    z, third = lax.shift_right_logical(rest, 2), lax.bitwise_and(rest, 3)
    x, y = jnp.where(core == 0, first, third), jnp.where(core == 0, third, first)
    return z * 96 + x * 24 + y * 6 + core * 3 + r


def chips_of(core, rest):
    second, third = lax.shift_right_logical(rest, 2), lax.bitwise_and(rest, 3)
    return jnp.where(core == 0, second * 4 + third, third * 4 + second)


def order_twelve(my_core):
    core, rest = own_first(my_core)
    r = lax.shift_right_logical(rest, 4)
    return chips_of(core, lax.bitwise_and(rest, 15)) * 24 + core * 12 + r


def order_six(core):
    p = iota((D, 1), 0)
    first = steps_of(p, 96, 4)
    rest = p - first * 96
    r = lax.shift_right_logical(rest, 4)
    rest = lax.bitwise_and(rest, 15)
    z, third = lax.shift_right_logical(rest, 2), lax.bitwise_and(rest, 3)
    x, y = jnp.where(core == 0, first, third), jnp.where(core == 0, third, first)
    return z * 192 + x * 48 + y * 12 + core * 6 + r


def turned(picks, columns):
    return mm_nt(picks, columns).astype(BF16)


def emit(tile, places):
    for at, (ref, first, q) in enumerate(places):
        ref[first, q] = tile[at * 16 : at * 16 + 16].astype(BF16)


def spots_three(refs, q_of):
    return [(ref, a, q_of(r)) for ref in refs for a in range(4) for r in range(3)]


def backward_mlp(my_core, upstream, gain_m, proj, up, down, store, keep, send):
    mixed_s, middle_s, second_s, hidden_s, slope_s = store
    both = (keep, send)
    down_in = upstream.astype(BF16)
    picks = pick(order_three(my_core))
    rows_up = turned(picks, second_s[...])
    picks_down = pick(order_twelve(my_core))
    second_grad = None
    stacked = jnp.concatenate([hidden_s[:, pl.ds(j * D, D)] for j in range(FF // D)], axis=0)
    rows = turned(picks_down, stacked)
    for j in range(FF // D):
        tile = mm(rows[:, j * ROWS : j * ROWS + ROWS], down_in)
        emit(tile, [(ref, j, r) for ref in both for r in range(12)])
    for j in range(FF // WIDE):
        cols = pl.ds(j * WIDE, WIDE)
        up_in = (slope_s[:, cols].astype(F32) * mm_nt(down_in, down[cols, :])).astype(BF16)
        tile = mm(rows_up, up_in)
        for i in range(WIDE // D):
            at = 12 + (j * (WIDE // D) + i) * 3
            emit(tile[:, i * D : i * D + D], spots_three(both, lambda r, at=at: at + r))
        part = mm_nt(up_in, up[:, cols])
        second_grad = part if second_grad is None else second_grad + part
    middle_grad = upstream + norm_pull(middle_s[...], gain_m, second_grad)
    proj_in = middle_grad.astype(BF16)
    emit(mm(turned(picks, mixed_s[...]), proj_in), spots_three(both, lambda r: 24 + r))
    return middle_grad, mm_nt(proj_in, proj[...]).astype(BF16)


def backward_attention(
    my_core, middle_grad, mixed_grad, stream_s, gain_a, qkv, store, wides, first_q, wide_s
):
    normed_s, triple_s, probs_s, mixed_s = store
    for pair in range(3):
        lanes = pl.ds(pair * 128, 128)
        q = triple_s[:, lanes] * 0.125
        k = triple_s[:, pl.ds(D + pair * 128, 128)]
        v = triple_s[:, pl.ds(2 * D + pair * 128, 128)]
        mg = mixed_grad[:, pair * 128 : pair * 128 + 128]
        product = mg.astype(F32) * mixed_s[:, lanes].astype(F32)
        dq = dk = dv = None
        for h in range(2):
            mask = head_mask(128, h)
            probs = probs_s[pair * 2 + h]
            mg_h = jnp.where(mask, mg, 0.0).astype(BF16)
            delta = jnp.sum(jnp.where(mask, product, 0.0), axis=-1, keepdims=True)
            probs_grad = mm_nt(mg_h, v)
            scores_grad = (probs.astype(F32) * (probs_grad - delta)).astype(BF16)
            part_q = mm(scores_grad, jnp.where(mask, k, 0.0).astype(BF16))
            part_k = mm_tn(scores_grad, jnp.where(mask, q, 0.0).astype(BF16))
            part_v = mm_tn(probs, mg_h)
            dq = part_q if dq is None else dq + part_q
            dk = part_k if dk is None else dk + part_k
            dv = part_v if dv is None else dv + part_v
        wide_s[:, lanes] = (dq * 0.125).astype(BF16)
        wide_s[:, pl.ds(D + pair * 128, 128)] = dk.astype(BF16)
        wide_s[:, pl.ds(2 * D + pair * 128, 128)] = dv.astype(BF16)
    rows_qkv = turned(pick(order_three(my_core)), normed_s[...])
    tile = mm(rows_qkv, wide_s[...])
    for j in range(3):
        emit(tile[:, j * D : j * D + D], spots_three(wides, lambda r, j=j: first_q + j * 3 + r))
    normed_grad = mm_nt(wide_s[...], qkv[...])
    return middle_grad + norm_pull(stream_s[...], gain_a, normed_grad)


def store_shapes():
    return [
        ((ROWS, D), BF16),
        ((ROWS, 3 * D), BF16),
        ((HEADS, ROWS, ROWS), BF16),
        ((ROWS, D), BF16),
        ((ROWS, D), F32),
        ((ROWS, D), BF16),
        ((ROWS, FF), BF16),
        ((ROWS, FF), BF16),
    ]


def whole(shape):
    return pl.BlockSpec(shape, lambda *_: (0,) * len(shape))


def shapes_of(items):
    return [jax.ShapeDtypeStruct(s, d) for s, d in items]


WEIGHTS = {
    "qkv": ((D, 3 * D), BF16),
    "proj": ((D, D), BF16),
    "up": ((D, FF), BF16),
    "down": ((FF, D), BF16),
}
STORES = dict(
    zip(
        ("normed", "triple", "probs", "mixed", "middle", "second", "hidden", "slope"),
        store_shapes(),
        strict=True,
    )
)
ANY_SPEC = pl.BlockSpec(memory_space=pl.ANY)
SCALARS = pl.BlockSpec(memory_space=pltpu.SMEM)
IN_VMEM = pl.BlockSpec(memory_space=pltpu.VMEM)
IN_HBM = pl.BlockSpec(memory_space=pltpu.HBM)


def gather_kernel(axis, *rest):
    pieces, out = rest[:4], rest[5]
    at = dict(zip("zxy", place_of_device()))[axis]
    for step, piece in zip((0, *STEPS), pieces, strict=True):
        out[lax.bitwise_and(at - step, 3)] = piece[...]


def gather_ring(axis, pieces, after):
    return local_kernel(
        partial(gather_kernel, axis),
        (*pieces, after),
        [((4, *pieces[0].shape), BF16)],
        [],
        "gather_ring",
    )[0]


def join_kernel(own, other, out):
    my_core = place_of_device()[3]
    out[my_core] = own[...]
    out[1 - my_core] = other[...]


def join_cores(own, other):
    return local_kernel(join_kernel, (own, other), [((2, 2, D), BF16)], [], "join_cores")[0]


def take_kernel(slot_of, _, *rest):
    pieces, (out, held_s) = rest[:4], rest[4:]
    z, x, y, my_core = place_of_device()
    for step, piece in zip((0, *STEPS), pieces, strict=True):
        held_s[lax.bitwise_and(y - step, 3)] = piece[...].astype(F32)
    device = z * 32 + x * 8 + y * 2 + my_core
    row = iota((2, 1), 0)
    taken = []
    for env in range(2):
        slot = slot_of[device * 2 + env]
        pair = held_s[
            lax.bitwise_and(lax.shift_right_logical(slot, 2), 3),
            lax.bitwise_and(lax.shift_right_logical(slot, 4), 3),
            lax.shift_right_logical(slot, 6),
            lax.bitwise_and(lax.shift_right_logical(slot, 1), 1),
        ]
        chosen = row == lax.bitwise_and(slot, 1)
        taken.append(jnp.sum(jnp.where(chosen, pair, 0.0), axis=0, keepdims=True))
    out[...] = jnp.where(row == 0, taken[0], taken[1])


def take_rows(slot_of, pieces, after):
    return pl.pallas_call(
        take_kernel,
        in_specs=[SCALARS, ANY_SPEC] + [IN_VMEM] * 4,
        out_specs=[IN_VMEM],
        out_shape=shapes_of([((2, D), F32)]),
        scratch_shapes=[pltpu.VMEM((4, 4, 4, 2, 2, D), F32)],
        compiler_params=pltpu.CompilerParams(vmem_limit_bytes=SMALL_VMEM_BYTES),
        name="take_rows",
    )(slot_of, after, *pieces)[0]


def big_kernel(kernel, operands, outs, scratch, flops, copies, name):
    return pl.pallas_call(
        kernel,
        in_specs=[spec for _, spec in operands],
        out_specs=[IN_VMEM for _ in outs],
        out_shape=shapes_of(outs),
        scratch_shapes=[(pltpu.VMEM if d != jnp.int32 else pltpu.SMEM)(s, d) for s, d in scratch]
        + [pltpu.SemaphoreType.DMA((copies,))] * (copies > 0),
        compiler_params=pltpu.CompilerParams(vmem_limit_bytes=VMEM_BYTES),
        cost_estimate=pl.CostEstimate(flops=flops, bytes_accessed=8000000, transcendentals=0),
        name=name,
    )(*[v for v, _ in operands])


def in_hbm(value):
    return pltpu.with_memory_space_constraint(value, pltpu.HBM)


def embed_kernel(
    counts, images, patch_weight, pos, gain_a, qkv, proj, gain_m, up, down, final_gain, *rest
):
    rows_o, stream_o, store, held, gains = rest[0], rest[1], rest[2:7], rest[7:11], rest[11:14]
    counts_o, flat_s, images_s, patch_s, pos_s, sems = rest[14:]
    first_copies = [
        pltpu.make_async_copy(source, target, sems.at[8 + at])
        for at, (source, target) in enumerate(
            (
                (images, images_s),
                (counts, counts_o),
                (patch_weight, patch_s),
                (pos, pos_s),
                (gain_a, gains[0]),
                (gain_m, gains[1]),
                (final_gain, gains[2]),
            )
        )
    ]
    copies = {}
    for layer in range(2):
        for at, (source, target) in enumerate(zip((qkv, proj, up, down), held, strict=True)):
            copies[layer, at] = pltpu.make_async_copy(
                source.at[layer], target.at[layer], sems.at[layer * 4 + at]
            )
    for copy in first_copies + list(copies.values()):
        copy.start()
    first_copies[0].wait()
    for env in range(2):
        for patch in range(PATCHES):
            at = (env * PATCHES + patch) * CAMS
            flat_s[pl.ds(at, CAMS)] = images_s[env, patch].astype(F32)
    first_copies[1].wait()
    first, second = counts_o[0], counts_o[1]
    row = iota((ROWS, 1), 0)
    cam = steps_of(row, PATCHES, CAM_MOST + 1)
    patch = row - cam * PATCHES
    slot = jnp.where(cam < first, cam, CAMS * PATCHES + cam - first)
    used = cam < first + second
    source = jnp.where(used, slot + patch * CAMS, -1)
    rows = mm(
        jnp.where(source == iota((ROWS, SLOTS * PATCHES), 1), 1.0, 0.0).astype(BF16),
        flat_s[...].astype(BF16),
    ).astype(BF16)
    rows_o[...] = rows
    place = jnp.where(used & (patch == iota((ROWS, PATCHES), 1)), 1.0, 0.0).astype(BF16)
    for copy in first_copies[2:]:
        copy.wait()
    stream = mm(rows, patch_s[...]) + mm(place, pos_s[...])
    stream_o[...] = stream
    attention_half(
        stream,
        gains[0][0:1],
        held[0].at[0],
        held[1].at[0],
        store,
        lambda at: copies[0, at].wait(),
    )
    for key in ((0, 2), (0, 3), (1, 0), (1, 1), (1, 2), (1, 3)):
        copies[key].wait()


STORE_A = ("normed", "triple", "probs", "mixed", "middle")
STORE_M = ("second", "hidden", "slope")


def run_embed(counts, images, patch_weight, pos, params, final_gain):
    gain_a, qkv, proj, gain_m, up, down = params
    sources = (counts, images, patch_weight, pos, gain_a, qkv, proj, gain_m, up, down, final_gain)
    got = big_kernel(
        embed_kernel,
        [(in_hbm(v), IN_HBM) for v in sources],
        [((ROWS, PATCH_DIM), BF16), ((ROWS, D), F32)]
        + [STORES[k] for k in STORE_A]
        + [((2, *s), d) for s, d in WEIGHTS.values()]
        + [((2, D), F32), ((2, D), F32), ((D,), F32)],
        [
            ((2,), jnp.int32),
            ((SLOTS * PATCHES, PATCH_DIM), F32),
            (images.shape, BF16),
            ((PATCH_DIM, D), BF16),
            ((PATCHES, D), BF16),
        ],
        7000000000,
        15,
        "embed_attend",
    )
    gain_a, gain_m, final_gain = got[11:14]
    params = (gain_a, *got[7:9], gain_m, *got[9:11])
    return got[0], got[1], dict(zip(STORE_A, got[2:7])), params, final_gain


def middle_kernel(middle, gain_a, gain_m, up, down, qkv, proj, _, *rest):
    stream_o, store_m, store_a = rest[0], rest[1:4], rest[4:9]
    stream_o[...] = mlp_half(middle[...], gain_m[0:1], up.at[0], down.at[0], store_m)
    attention_half(
        stream_o[...], gain_a[1:2], qkv.at[1], proj.at[1], store_a, lambda at: None
    )


def run_middle(middle, params, after):
    gain_a, qkv, proj, gain_m, up, down = params
    got = big_kernel(
        middle_kernel,
        [(v, IN_VMEM) for v in (middle, gain_a, gain_m, up, down, qkv, proj)] + [(after, ANY_SPEC)],
        [((ROWS, D), F32)] + [STORES[k] for k in STORE_M + STORE_A],
        [],
        6000000000,
        0,
        "mlp_attend",
    )
    return got[0], dict(zip(STORE_M, got[1:4])), dict(zip(STORE_A, got[4:9]))


def pool_kernel(counts, middle, gain_m, up, down, final_gain, _, *rest):
    pooled_o, tokens_o, store_m = rest[0], rest[1], rest[2:5]
    last = mlp_half(middle[...], gain_m[1:2], up.at[1], down.at[1], store_m)
    pooled = exact_mm(camera_members(), last) * (1.0 / PATCHES)
    pooled_o[...] = pooled
    embedded = norm_rows(pooled, final_gain[...][None])
    first, second = counts[0], counts[1]
    cam = iota((SLOTS, 1), 0)
    in_first = cam < first
    in_second = (cam >= first) & (cam < first + second)
    sum_first = jnp.sum(jnp.where(in_first, embedded, 0.0), axis=0, keepdims=True)
    sum_second = jnp.sum(jnp.where(in_second, embedded, 0.0), axis=0, keepdims=True)
    row = iota((SLOTS, 1), 0)
    count_col = jnp.where(row == 0, first, second).astype(F32)
    both = jnp.where(row == 0, sum_first, jnp.where(row == 1, sum_second, 0.0))
    tokens_o[...] = (both / count_col).astype(BF16)


def run_pool(counts, middle, params, final_gain, after):
    _, _, _, gain_m, up, down = params
    got = big_kernel(
        pool_kernel,
        [(counts, SCALARS)]
        + [(v, IN_VMEM) for v in (middle, gain_m, up, down, final_gain)]
        + [(after, ANY_SPEC)],
        [((SLOTS, D), F32), ((SLOTS, D), BF16)] + [STORES[k] for k in STORE_M],
        [],
        4000000000,
        0,
        "mlp_pool",
    )
    return got[0], got[1], dict(zip(STORE_M, got[2:5]))


def camera_members():
    cam = steps_of(iota((1, ROWS), 1), PATCHES, CAM_MOST + 1)
    return jnp.where(cam == iota((SLOTS, 1), 0), 1.0, 0.0)


GRAD_COUNTS = {"second": (12, 24), "first_mlp": (12, 15), "first_attention": (0, 17)}


ROWS_D, ROWS_W = (sum(n) for n in zip(*GRAD_COUNTS.values()))


def grad_shapes(group):
    return [((4, sum(GRAD_COUNTS[group]), 16, D), BF16)] * 2


def place_of_device():
    env = lax.axis_index("env")
    return (
        lax.axis_index("grp"),
        lax.shift_right_logical(env, 3),
        lax.bitwise_and(lax.shift_right_logical(env, 1), 3),
        lax.bitwise_and(env, 1),
    )


SECOND_IN = ("second", "hidden", "down", "slope", "up", "middle", "mixed", "proj")
ATTENTION_IN = ("triple", "probs", "normed", "qkv")


def of_layer(names, refs, layer):
    refs = dict(zip(names, refs))
    return {key: ref.at[layer] if key in WEIGHTS else ref for key, ref in refs.items()}


def back_second_kernel(counts, seeds, pooled, final_gain, gain_a, gain_m, *rest):
    names = SECOND_IN + ATTENTION_IN + ("stream",)
    held, rest = of_layer(names, rest, 1), rest[len(names) :]
    keep, send, grad_o, wide_s = rest
    my_core = place_of_device()[3]
    first, second = counts[0], counts[1]
    cam = iota((SLOTS, 1), 0)
    seed = jnp.where(
        cam < first,
        seeds[0:1] / first.astype(F32),
        jnp.where(cam < first + second, seeds[1:2] / second.astype(F32), 0.0),
    )
    pooled_grad = norm_pull(pooled[...], final_gain[...][None], seed) * (1.0 / PATCHES)
    cam_row = steps_of(iota((ROWS, 1), 0), PATCHES, CAM_MOST + 1)
    member = jnp.where(cam_row == iota((1, SLOTS), 1), 1.0, 0.0)
    upstream = exact_mm(member, pooled_grad)
    middle_grad, mixed_grad = backward_mlp(
        my_core,
        upstream,
        gain_m[1:2],
        held["proj"],
        held["up"],
        held["down"],
        [held[k] for k in ("mixed", "middle", "second", "hidden", "slope")],
        keep,
        send,
    )
    grad_o[...] = backward_attention(
        my_core,
        middle_grad,
        mixed_grad,
        held["stream"],
        gain_a[1:2],
        held["qkv"],
        [held[k] for k in ("normed", "triple", "probs", "mixed")],
        (keep, send),
        27,
        wide_s,
    )


def run_back_second(counts, seeds, pooled, final_gain, stream, params, store):
    gain_a, qkv, proj, gain_m, up, down = params
    values = {"qkv": qkv, "proj": proj, "up": up, "down": down, "stream": stream}
    values.update(store)
    names = SECOND_IN + ATTENTION_IN + ("stream",)
    return big_kernel(
        back_second_kernel,
        [(counts, SCALARS)]
        + [(v, IN_VMEM) for v in (seeds, pooled, final_gain, gain_a, gain_m)]
        + [(values[k], IN_VMEM) for k in names],
        grad_shapes("second") + [((ROWS, D), F32)],
        [((ROWS, 3 * D), BF16)],
        8000000000,
        0,
        "back_second",
    )


def back_mlp_kernel(gain_m, *rest):
    names = ("stream",) + SECOND_IN
    held, rest = of_layer(names, rest, 0), rest[len(names) :]
    keep, send, middle_o, mixed_o = rest
    middle_o[...], mixed_o[...] = backward_mlp(
        place_of_device()[3],
        held["stream"][...],
        gain_m[0:1],
        held["proj"],
        held["up"],
        held["down"],
        [held[k] for k in ("mixed", "middle", "second", "hidden", "slope")],
        keep,
        send,
    )


def run_back_mlp(upstream, params, store):
    _, _, proj, gain_m, up, down = params
    values = {"proj": proj, "up": up, "down": down, "stream": upstream}
    values.update(store)
    names = ("stream",) + SECOND_IN
    return big_kernel(
        back_mlp_kernel,
        [(gain_m, IN_VMEM)] + [(values[k], IN_VMEM) for k in names],
        grad_shapes("first_mlp") + [((ROWS, D), F32), ((ROWS, D), BF16)],
        [],
        5000000000,
        0,
        "back_first_mlp",
    )


def back_attention_kernel(slot_of, tokens, middle_grad, mixed_grad, gain_a, *rest):
    names = ("mixed",) + ATTENTION_IN + ("stream", "rows")
    held, rest = of_layer(names, rest, 0), rest[len(names) :]
    keep, send, wide_s = rest
    z, x, y, my_core = place_of_device()
    device = z * 32 + x * 8 + y * 2 + my_core
    p = iota((ROWS, 1), 0)
    swap = jnp.where(p >= 128, 1, 0)
    core = jnp.where(swap == my_core, 0, 1)
    rest_p = p - swap * 128
    first = lax.shift_right_logical(rest_p, 5)
    row = lax.bitwise_and(lax.shift_right_logical(rest_p, 4), 1)
    third = lax.bitwise_and(rest_p, 3)
    to_x, to_y = jnp.where(core == 0, first, third), jnp.where(core == 0, third, first)
    to_z = lax.bitwise_and(lax.shift_right_logical(rest_p, 2), 3)
    learner = to_z * 64 + to_x * 16 + to_y * 4 + core * 2 + row
    lane = iota((1, SLOTS), 1)
    wanted = jnp.where(
        lane == 0, slot_of[device * 2], jnp.where(lane == 1, slot_of[device * 2 + 1], -1)
    )
    spread = mm(jnp.where(learner == wanted, 1.0, 0.0).astype(BF16), tokens[...]).astype(BF16)
    spots = [(ref, a, r) for ref in (keep, send) for a in range(4) for r in range(2)]
    for at, (ref, a, r) in enumerate(spots):
        ref[a, 15 + r] = spread[at * 16 : at * 16 + 16]
    stream_grad = backward_attention(
        my_core,
        middle_grad[...],
        mixed_grad[...],
        held["stream"],
        gain_a[0:1],
        held["qkv"],
        [held[k] for k in ("normed", "triple", "probs", "mixed")],
        (keep, send),
        0,
        wide_s,
    ).astype(BF16)
    for ref, core in ((keep, my_core), (send, 1 - my_core)):
        tile = mm(turned(pick(order_six(core), PATCH_DIM), held["rows"][...]), stream_grad)
        emit(tile, [(ref, a, 9 + r) for a in range(4) for r in range(6)])


def run_back_attention(slot_of, tokens, middle_grad, mixed_grad, rows, stream, params, store):
    values = {"qkv": params[1], "stream": stream, "rows": rows}
    values.update(store)
    names = ("mixed",) + ATTENTION_IN + ("stream", "rows")
    return big_kernel(
        back_attention_kernel,
        [(slot_of, SCALARS)]
        + [(v, IN_VMEM) for v in (tokens, middle_grad, mixed_grad, params[0])]
        + [(values[k], IN_VMEM) for k in names],
        grad_shapes("first_attention"),
        [((ROWS, 3 * D), BF16)],
        4000000000,
        0,
        "back_first_attention",
    )


def local_kernel(kernel, operands, outs, scratch, name):
    return pl.pallas_call(
        kernel,
        in_specs=[IN_VMEM for _ in operands],
        out_specs=[IN_VMEM for _ in outs],
        out_shape=shapes_of(outs),
        scratch_shapes=scratch,
        compiler_params=pltpu.CompilerParams(vmem_limit_bytes=SMALL_VMEM_BYTES),
        name=name,
    )(*operands)


def add_kernel(*rest):
    parts, outs = rest[:-8], rest[-8:]
    z, x, y, my_core = place_of_device()
    along = jnp.where(my_core == 0, x, y)
    at_d = at_w = 0
    for group, (count_d, count_w) in enumerate(GRAD_COUNTS.values()):
        keep, got = parts[group * 2 : group * 2 + 2]
        for step in range(4):
            place_d, place_w = lax.bitwise_and(z + step, 3), lax.bitwise_and(along + step, 3)
            if count_d:
                span = pl.ds(0, count_d)
                outs[step][pl.ds(at_d, count_d)] = keep[place_d, span] + got[place_d, span]
            span = pl.ds(count_d, count_w)
            outs[4 + step][pl.ds(at_w, count_w)] = keep[place_w, span] + got[place_w, span]
        at_d, at_w = at_d + count_d, at_w + count_w


def add_pairs(*parts):
    return local_kernel(
        add_kernel,
        parts,
        [((ROWS_D, 16, D), BF16)] * 4 + [((ROWS_W, 16, D), BF16)] * 4,
        [],
        "add_pairs",
    )


def sum_of(refs):
    total = refs[0][...].astype(F32)
    for ref in refs[1:]:
        total = total + ref[...].astype(F32)
    return total


def place_on(axes):
    z, x, y, my_core = place_of_device()
    by_name = {"z": z, "x": x, "y": y}
    return jnp.where(my_core == 0, by_name[axes[0]], by_name[axes[1]])


def first_sum_kernel(axes, *rest):
    parts, outs, (total_s, turn_s) = rest[:4], rest[4:8], rest[8:]
    count = parts[0].shape[0]
    total = sum_of(parts).reshape(count * 16, D)
    for lanes in range(3):
        total_s[lanes] = total[:, lanes * 128 : lanes * 128 + 128]
    for b in range(16):
        for lanes in range(3):
            turn_s[b // 4, pl.ds(b % 4 * count, count), pl.ds(lanes * 128, 128)] = total_s[
                lanes, pl.ds(b, count, 16)
            ]
    along = place_on(axes)
    for step in range(4):
        outs[step][...] = turn_s[lax.bitwise_and(along + step, 3)].astype(BF16)


def first_sum(axes, parts):
    count = parts[0].shape[0]
    return local_kernel(
        partial(first_sum_kernel, axes),
        parts,
        [((4 * count, D), BF16)] * 4,
        [pltpu.VMEM((3, count * 16, 128), F32), pltpu.VMEM((4, 4 * count, D), F32)],
        "first_sum",
    )


def wide_sum_kernel(*rest):
    rest[4][...] = sum_of(rest[:4])


def wide_sum(parts):
    return local_kernel(wide_sum_kernel, parts, [((4 * ROWS_W, D), F32)], [], "wide_sum")


def second_sum_kernel(*rest):
    parts, wide, outs, total_s = rest[:4], rest[4], rest[5:9], rest[9]
    total_d, total_w = sum_of(parts), wide[...]
    for third in range(4):
        total_s[third, pl.ds(0, ROWS_D)] = total_d[third * ROWS_D : (third + 1) * ROWS_D]
        total_s[third, pl.ds(ROWS_D, ROWS_W)] = total_w[third * ROWS_W : (third + 1) * ROWS_W]
    _, x, y, my_core = place_of_device()
    along = jnp.where(my_core == 0, y, x)
    for step in range(4):
        outs[step][...] = total_s[lax.bitwise_and(along + step, 3)].astype(BF16)


def second_sum(parts):
    return local_kernel(
        second_sum_kernel,
        parts,
        [((ROWS_D + ROWS_W, D), BF16)] * 4,
        [pltpu.VMEM((4, ROWS_D + ROWS_W, D), F32)],
        "second_sum",
    )


def last_sum_kernel(*rest):
    parts, (tokens, patch, qkv, proj, up, down) = rest[:4], rest[4:]
    rows = sum_of(parts)
    down[:, 1], down[:, 0] = rows[0:12], rows[12:24]
    wide = rows[ROWS_D:]
    for layer, at_up, at_qkv in ((1, 0, 15), (0, 24, 39)):
        for j in range(4):
            up[:, layer, pl.ds(j * D, D)] = wide[at_up + j * 3 : at_up + j * 3 + 3]
        proj[:, layer] = wide[at_up + 12 : at_up + 15]
        for j in range(3):
            qkv[:, layer, pl.ds(j * D, D)] = wide[at_qkv + j * 3 : at_qkv + j * 3 + 3]
    patch[...] = wide[48:54]
    tokens[...] = wide[54:56].astype(BF16)


def last_sum(parts):
    return local_kernel(
        last_sum_kernel,
        parts,
        [
            ((2, D), BF16),
            ((6, D), F32),
            ((3, 2, 3 * D), F32),
            ((3, 2, D), F32),
            ((3, 2, FF), F32),
            ((12, 2, D), F32),
        ],
        [],
        "last_sum",
    )


AXES = ("grp", "env")
STEPS = (2, 1, 3)


def send_along(value, axes, step):
    pairs = []
    for device in range(128):
        z, x, y, core = device // 32, device // 8 % 4, device // 2 % 4, device % 2
        place = {"z": z, "x": x, "y": y}
        place[axes[core]] = (place[axes[core]] + step) % 4
        pairs.append((device, place["z"] * 32 + place["x"] * 8 + place["y"] * 2 + core))
    return lax.ppermute(value, AXES, pairs)


def swap_cores(value):
    return lax.ppermute(value, AXES, [(device, device ^ 1) for device in range(128)])


def exchange(pieces, axes):
    return [pieces[0]] + [send_along(pieces[step], axes, step) for step in STEPS]


def per_device(
    images,
    camera_counts,
    slot_of,
    patch_weight,
    pos_embed,
    attn_gain,
    qkv_weight,
    proj_weight,
    mlp_gain,
    up_weight,
    down_weight,
    final_gain,
    cotangent,
):
    params = (attn_gain, qkv_weight, proj_weight, mlp_gain, up_weight, down_weight)
    chip = join_cores(cotangent, swap_cores(cotangent))
    ring = exchange([chip] * 4, "zz")
    rows, stream, store_first, params, final_gain = run_embed(
        camera_counts,
        jnp.swapaxes(images, 1, 2),
        patch_weight,
        pos_embed,
        params,
        final_gain,
    )
    line = gather_ring("z", ring, final_gain)
    ring = exchange([line] * 4, "xx")
    middle_stream, store, store_second = run_middle(store_first["middle"], params, line)
    store_first.update(store)
    plane = gather_ring("x", ring, store["second"])
    ring = exchange([plane] * 4, "yy")
    pooled, tokens, store = run_pool(
        camera_counts, store_second["middle"], params, final_gain, plane
    )
    store_second.update(store)
    seeds = take_rows(slot_of, ring, pooled)
    keep_second, send, stream_grad = run_back_second(
        camera_counts,
        seeds,
        pooled,
        final_gain,
        middle_stream,
        params,
        store_second,
    )
    got_second = swap_cores(send)
    keep_mlp, send, middle_grad, mixed_grad = run_back_mlp(stream_grad, params, store_first)
    got_mlp = swap_cores(send)
    keep, send = run_back_attention(
        slot_of,
        tokens,
        middle_grad,
        mixed_grad,
        rows,
        stream,
        params,
        store_first,
    )
    got = swap_cores(send)
    pieces = add_pairs(keep_second, got_second, keep_mlp, got_mlp, keep, got)
    wide = exchange(pieces[4:], "xy")
    deep = exchange(pieces[:4], "zz")
    wide = exchange(first_sum("zz", wide), "zz")
    deep = exchange(first_sum("xy", deep), "xy")
    pieces = second_sum([*deep, *wide_sum(wide)])
    tokens, patch, *stacks = last_sum(exchange(pieces, "yx"))
    return (tokens, patch, *(jnp.swapaxes(stack, 0, 1) for stack in stacks))


def solution(mesh):
    placed = (
        P(("grp", "env"), None, None, None),
        P(("grp", "env")),
        P(),
        P(),
        P(),
        P(),
        P(),
        P(),
        P(),
        P(),
        P(),
        P(),
        P(("grp", "env"), None),
    )
    return jax.shard_map(
        per_device,
        mesh=mesh,
        in_specs=placed,
        out_specs=(
            P(("grp", "env"), None),
            P(("grp", "env"), None),
            P(None, ("grp", "env"), None),
            P(None, ("grp", "env"), None),
            P(None, ("grp", "env"), None),
            P(None, ("grp", "env"), None),
        ),
        check_vma=False,
    )
```

profile of v0, /device:TPU:0, one launch (start us, length us, event | category | flops | bytes accessed | tf_op | source)
XLA Modules:
  0.0 92.1 jit_solution(5842312922495905406)
XLA Ops:
  0.7 1.3 %collective-permute-done.other = bf16[2,384]{1,0:T(2,128)(2,1)S(1)} collective-permute-done((bf16[2,384]{1,0:T(2,128)(2,1)}, bf16[2,384]{1,0:T(2,128)(2,1)S(1)}, u32[]{:S(2)}, u32[]{:S(2)}) %collective-permute-start) | collective-permute-done | bytes 1568 | tf_op jit(solution)/shard_map/ppermute | solution.py:864
  2.8 4.1 %collective-permute-start.3 = (bf16[2,2,384]{2,1,0:T(2,128)(2,1)S(1)}, bf16[2,2,384]{2,1,0:T(2,128)(2,1)S(1)}, u32[]{:S(2)}, u32[]{:S(2)}) collective-permute-start(bf16[2,2,384]{2,1,0:T(2,128)(2,1)S(1)} %join_cores.1.rest_0_), channel_id=1, source_target_pairs={{0,96},{1,97},{2,98},{3,99},{4,100},{5,101},{6,102},{7,103},{8,104... | collective-permute-start | bytes 9224 | tf_op jit(solution)/shard_map/ppermute | solution.py:860
  6.9 1.9 %collective-permute-start.1 = (bf16[2,2,384]{2,1,0:T(2,128)(2,1)S(1)}, bf16[2,2,384]{2,1,0:T(2,128)(2,1)S(1)}, u32[]{:S(2)}, u32[]{:S(2)}) collective-permute-start(bf16[2,2,384]{2,1,0:T(2,128)(2,1)S(1)} %join_cores.1.rest_0_), channel_id=1, source_target_pairs={{0,64},{1,65},{2,66},{3,67},{4,68},{5,69},{6,70},{7,71},{8,72},{9,... | collective-permute-start | bytes 9224 | tf_op jit(solution)/shard_map/ppermute | solution.py:860
  8.7 4.1 %embed_attend.1 = (bf16[256,768]{1,0:T(8,128)(2,1)S(1)}, f32[256,384]{1,0:T(8,128)S(1)}, bf16[256,384]{1,0:T(8,128)(2,1)S(1)}, bf16[256,1152]{1,0:T(8,128)(2,1)S...) custom-call(s32[2]{0:T(128)} %counts.5, ...), custom_call_target="tpu_custom_call" | custom-call | flops 7000000000 | bytes 8000000 | tf_op jit(solution)/shard_map/embed_attend/pallas_call | solution.py:359
  12.9 2.8 %collective-permute-start.6 = (bf16[4,2,2,384]{3,2,1,0:T(2,128)(2,1)S(1)}, bf16[4,2,2,384]{3,2,1,0:T(2,128)(2,1)S(1)}, u32[]{:S(2)}, u32[]{:S(2)}) collective-permute-start(bf16[4,2,2,384]{3,2,1,0:T(2,128)(2,1)S(1)} %gather_ring.2._.rest_0_), channel_id=1, source_target_pairs={{0,24},{1,25},{2,26},{3,27},{4,28},{5,29},{6,30},{7,31},{8,0},{9,1... | collective-permute-start | bytes 36872 | tf_op jit(solution)/shard_map/ppermute | solution.py:860
  15.7 2.3 %collective-permute-start.4 = (bf16[4,2,2,384]{3,2,1,0:T(2,128)(2,1)S(1)}, bf16[4,2,2,384]{3,2,1,0:T(2,128)(2,1)S(1)}, u32[]{:S(2)}, u32[]{:S(2)}) collective-permute-start(bf16[4,2,2,384]{3,2,1,0:T(2,128)(2,1)S(1)} %gather_ring.2._.rest_0_), channel_id=1, source_target_pairs={{0,16},{1,17},{2,18},{3,19},{4,20},{5,21},{6,22},{7,23},{8,24},{9,... | collective-permute-start | bytes 36872 | tf_op jit(solution)/shard_map/ppermute | solution.py:860
  18.0 3.9 %mlp_attend.1 = (f32[256,384]{1,0:T(8,128)S(1)}, bf16[256,384]{1,0:T(8,128)(2,1)S(1)}, bf16[256,1536]{1,0:T(8,128)(2,1)S(1)}, bf16[256,1536]{1,0:T(8,128)(2,1)S(...) custom-call(f32[256,384]{1,0:T(8,128)S(1)} %get-tuple-element.69.mid, ...), custom_call_target="tpu_custom_call" | custom-call | flops 6000000000 | bytes 8000000 | tf_op jit(solution)/shard_map/mlp_attend/pallas_call | solution.py:359
  21.9 3.1 %collective-permute-start.9 = (bf16[4,4,2,2,384]{4,3,2,1,0:T(2,128)(2,1)S(1)}, bf16[4,4,2,2,384]{4,3,2,1,0:T(2,128)(2,1)S(1)}, u32[]{:S(2)}, u32[]{:S(2)}) collective-permute-start(bf16[4,4,2,2,384]{4,3,2,1,0:T(2,128)(2,1)S(1)} %gather_ring.3._.rest_0_), channel_id=1, source_target_pairs={{0,6},{1,7},{2,0},{3,1},{4,2},{5,3},{6,4},{7,5},{8,14},{9,15},{10,... | collective-permute-start | bytes 147464 | tf_op jit(solution)/shard_map/ppermute | solution.py:860
  25.0 2.2 %collective-permute-start.7 = (bf16[4,4,2,2,384]{4,3,2,1,0:T(2,128)(2,1)S(1)}, bf16[4,4,2,2,384]{4,3,2,1,0:T(2,128)(2,1)S(1)}, u32[]{:S(2)}, u32[]{:S(2)}) collective-permute-start(bf16[4,4,2,2,384]{4,3,2,1,0:T(2,128)(2,1)S(1)} %gather_ring.3._.rest_0_), channel_id=1, source_target_pairs={{0,4},{1,5},{2,6},{3,7},{4,0},{5,1},{6,2},{7,3},{8,12},{9,13},{10,... | collective-permute-start | bytes 147464 | tf_op jit(solution)/shard_map/ppermute | solution.py:860
  27.2 3.1 %mlp_pool.1 = (f32[8,384]{1,0:T(8,128)S(1)}, bf16[8,384]{1,0:T(8,128)(2,1)S(1)}, bf16[256,384]{1,0:T(8,128)(2,1)S(1)}, bf16[256,1536]{1,0:T(8,128)(2,1)S(1)}, bf16[256,1536]{1,0:T(8,128)(2,1)S(1)}) custom-call(s32[2]{0:T(128)S(1)} %copy-done.2, f32[256,384]{1,0:T(8,128)S(1)} %get-tuple-element.77.middle.rest_5_, f32[2,384]{1,0:T(2,128)S(1)} %get-tuple-element.71.gain_m, ...), custom_call_target="tpu_custom_call" | custom-call | flops 4000000000 | bytes 8000000 | tf_op jit(solution)/shard_map/mlp_pool/pallas_call | solution.py:359
  31.5 6.2 %back_second.1 = (bf16[4,36,16,384]{3,2,1,0:T(8,128)(2,1)S(1)}, bf16[4,36,16,384]{3,2,1,0:T(8,128)(2,1)S(1)}, f32[256,384]{1,0:T(8,128)S(1)}) custom-call(s32[2]{0:T(128)S(1)} %copy-done.2, f32[2,384]{1,0:T(2,128)S(1)} %take_rows.1.seeds, f32[8,384]{1,0:T(8,128)S(1)} %get-tuple-element.79._.pooled, f32[384]{0:T(512)S(1)} %get-tuple-element.76.rest_4_.final_gain, ...), custom_call_target="tpu_custom_call" | custom-call | flops 8000000000 | bytes 8000000 | tf_op jit(solution)/shard_map/back_second/pallas_call | solution.py:359
  37.8 3.2 %back_first_mlp.1 = (bf16[4,27,16,384]{3,2,1,0:T(8,128)(2,1)S(1)}, bf16[4,27,16,384]{3,2,1,0:T(8,128)(2,1)S(1)}, f32[256,384]{1,0:T(8,128)S(1)}, bf16[256,384]{1,0:T(8,128)(2,1)S(1)}) custom-call(f32[2,384]{1,0:T(2,128)S(1)} %get-tuple-element.71.gain_m, f32[256,384]{1,0:T(8,128)S(1)} %get-tuple-element.90.rest_0_, ...), custom_call_target="tpu_custom_call" | custom-call | flops 5000000000 | bytes 8000000 | tf_op jit(solution)/shard_map/back_first_mlp/pallas_call | solution.py:359
  41.8 3.9 %back_first_attention.1 = (bf16[4,17,16,384]{3,2,1,0:T(8,128)(2,1)S(1)}, bf16[4,17,16,384]{3,2,1,0:T(8,128)(2,1)S(1)}) custom-call(s32[256]{0:T(256)S(1)} %copy-done.1, bf16[8,384]{1,0:T(8,128)(2,1)S(1)} %get-tuple-element.96.tokens, f32[256,384]{1,0:T(8,128)S(1)} %get-tuple-element.97.middle_grad, bf16[256,384]{1,0:T(8,128)(2,1)S(1)} %get-tuple-element.98.mixed_grad, ...), custom_call_target="tpu_custom_call" | custom-call | flops 4000000000 | bytes 8000000 | tf_op jit(solution)/shard_map/back_first_attention/pallas_call | solution.py:359
  45.8 2.3 %collective-permute-done.12.rest_5_ = bf16[4,17,16,384]{3,2,1,0:T(8,128)(2,1)S(1)} collective-permute-done((bf16[4,17,16,384]{3,2,1,0:T(8,128)(2,1)S(1)}, bf16[4,17,16,384]{3,2,1,0:T(8,128)(2,1)S(1)}, u32[]{:S(2)}, u32[]{:S(2)}) %collective-permute-start.12) | collective-permute-done | bytes 835616 | tf_op jit(solution)/shard_map/ppermute | solution.py:864
  48.7 1.4 %collective-permute-start.19 = (bf16[56,16,384]{2,1,0:T(8,128)(2,1)S(1)}, bf16[56,16,384]{2,1,0:T(8,128)(2,1)S(1)}, u32[]{:S(2)}, u32[]{:S(2)}) collective-permute-start(bf16[56,16,384]{2,1,0:T(8,128)(2,1)S(1)} %get-tuple-element.115), channel_id=1, source_target_pairs={{0,16},{1,5},{2,18},{3,7},{4,20},{5,1},{6,22},{7,3},{8,24},{9,13},... | collective-permute-start | bytes 2064392 | tf_op jit(solution)/shard_map/ppermute | solution.py:860
  50.1 1.8 %collective-permute-start.20 = (bf16[56,16,384]{2,1,0:T(8,128)(2,1)S(1)}, bf16[56,16,384]{2,1,0:T(8,128)(2,1)S(1)}, u32[]{:S(2)}, u32[]{:S(2)}) collective-permute-start(bf16[56,16,384]{2,1,0:T(8,128)(2,1)S(1)} %get-tuple-element.116), channel_id=1, source_target_pairs={{0,8},{1,3},{2,10},{3,5},{4,12},{5,7},{6,14},{7,1},{8,16},{9,11},{... | collective-permute-start | bytes 2064392 | tf_op jit(solution)/shard_map/ppermute | solution.py:860
  51.9 1.4 %collective-permute-start.21 = (bf16[56,16,384]{2,1,0:T(8,128)(2,1)S(1)}, bf16[56,16,384]{2,1,0:T(8,128)(2,1)S(1)}, u32[]{:S(2)}, u32[]{:S(2)}) collective-permute-start(bf16[56,16,384]{2,1,0:T(8,128)(2,1)S(1)} %get-tuple-element.117), channel_id=1, source_target_pairs={{0,24},{1,7},{2,26},{3,1},{4,28},{5,3},{6,30},{7,5},{8,0},{9,15},{... | collective-permute-start | bytes 2064392 | tf_op jit(solution)/shard_map/ppermute | solution.py:860
  53.3 1.7 %collective-permute-start.13 = (bf16[24,16,384]{2,1,0:T(8,128)(2,1)S(1)}, bf16[24,16,384]{2,1,0:T(8,128)(2,1)S(1)}, u32[]{:S(2)}, u32[]{:S(2)}) collective-permute-start(bf16[24,16,384]{2,1,0:T(8,128)(2,1)S(1)} %get-tuple-element.107), channel_id=1, source_target_pairs={{0,64},{1,65},{2,66},{3,67},{4,68},{5,69},{6,70},{7,71},{8,72},{9,... | collective-permute-start | bytes 884744 | tf_op jit(solution)/shard_map/ppermute | solution.py:860
  55.0 1.5 %collective-permute-start.14 = (bf16[24,16,384]{2,1,0:T(8,128)(2,1)S(1)}, bf16[24,16,384]{2,1,0:T(8,128)(2,1)S(1)}, u32[]{:S(2)}, u32[]{:S(2)}) collective-permute-start(bf16[24,16,384]{2,1,0:T(8,128)(2,1)S(1)} %get-tuple-element.108), channel_id=1, source_target_pairs={{0,32},{1,33},{2,34},{3,35},{4,36},{5,37},{6,38},{7,39},{8,40},{9,... | collective-permute-start | bytes 884744 | tf_op jit(solution)/shard_map/ppermute | solution.py:860
  56.4 4.9 %collective-permute-done.19.rest_1_ = bf16[56,16,384]{2,1,0:T(8,128)(2,1)S(1)} collective-permute-done((bf16[56,16,384]{2,1,0:T(8,128)(2,1)S(1)}, bf16[56,16,384]{2,1,0:T(8,128)(2,1)S(1)}, u32[]{:S(2)}, u32[]{:S(2)}) %collective-permute-start.19) | collective-permute-done | bytes 688160 | tf_op jit(solution)/shard_map/ppermute | solution.py:860
  61.3 2.3 %collective-permute-start.15 = (bf16[24,16,384]{2,1,0:T(8,128)(2,1)S(1)}, bf16[24,16,384]{2,1,0:T(8,128)(2,1)S(1)}, u32[]{:S(2)}, u32[]{:S(2)}) collective-permute-start(bf16[24,16,384]{2,1,0:T(8,128)(2,1)S(1)} %get-tuple-element.109), channel_id=1, source_target_pairs={{0,96},{1,97},{2,98},{3,99},{4,100},{5,101},{6,102},{7,103},{8,104... | collective-permute-start | bytes 884744 | tf_op jit(solution)/shard_map/ppermute | solution.py:860
  63.6 5.0 %collective-permute-done.20.rest_2_ = bf16[56,16,384]{2,1,0:T(8,128)(2,1)S(1)} collective-permute-done((bf16[56,16,384]{2,1,0:T(8,128)(2,1)S(1)}, bf16[56,16,384]{2,1,0:T(8,128)(2,1)S(1)}, u32[]{:S(2)}, u32[]{:S(2)}) %collective-permute-start.20) | collective-permute-done | bytes 688160 | tf_op jit(solution)/shard_map/ppermute | solution.py:860
  69.7 1.8 %collective-permute-start.22 = (bf16[224,384]{1,0:T(8,128)(2,1)S(1)}, bf16[224,384]{1,0:T(8,128)(2,1)S(1)}, u32[]{:S(2)}, u32[]{:S(2)}) collective-permute-start(bf16[224,384]{1,0:T(8,128)(2,1)S(1)} %get-tuple-element.119), channel_id=1, source_target_pairs={{0,64},{1,65},{2,66},{3,67},{4,68},{5,69},{6,70},{7,71},{8,72},{9,... | collective-permute-start | bytes 516104 | tf_op jit(solution)/shard_map/ppermute | solution.py:860
  71.4 1.4 %collective-permute-start.23 = (bf16[224,384]{1,0:T(8,128)(2,1)S(1)}, bf16[224,384]{1,0:T(8,128)(2,1)S(1)}, u32[]{:S(2)}, u32[]{:S(2)}) collective-permute-start(bf16[224,384]{1,0:T(8,128)(2,1)S(1)} %get-tuple-element.120), channel_id=1, source_target_pairs={{0,32},{1,33},{2,34},{3,35},{4,36},{5,37},{6,38},{7,39},{8,40},{9,... | collective-permute-start | bytes 516104 | tf_op jit(solution)/shard_map/ppermute | solution.py:860
  72.9 1.8 %collective-permute-start.24 = (bf16[224,384]{1,0:T(8,128)(2,1)S(1)}, bf16[224,384]{1,0:T(8,128)(2,1)S(1)}, u32[]{:S(2)}, u32[]{:S(2)}) collective-permute-start(bf16[224,384]{1,0:T(8,128)(2,1)S(1)} %get-tuple-element.121), channel_id=1, source_target_pairs={{0,96},{1,97},{2,98},{3,99},{4,100},{5,101},{6,102},{7,103},{8,104... | collective-permute-start | bytes 516104 | tf_op jit(solution)/shard_map/ppermute | solution.py:860
  75.1 2.5 %collective-permute-start.16 = (bf16[96,384]{1,0:T(8,128)(2,1)S(1)}, bf16[96,384]{1,0:T(8,128)(2,1)S(1)}, u32[]{:S(2)}, u32[]{:S(2)}) collective-permute-start(bf16[96,384]{1,0:T(8,128)(2,1)S(1)} %get-tuple-element.111), channel_id=1, source_target_pairs={{0,16},{1,5},{2,18},{3,7},{4,20},{5,1},{6,22},{7,3},{8,24},{9,13},... | collective-permute-start | bytes 221192 | tf_op jit(solution)/shard_map/ppermute | solution.py:860
  78.3 2.6 %collective-permute-start.18 = (bf16[96,384]{1,0:T(8,128)(2,1)S(1)}, bf16[96,384]{1,0:T(8,128)(2,1)S(1)}, u32[]{:S(2)}, u32[]{:S(2)}) collective-permute-start(bf16[96,384]{1,0:T(8,128)(2,1)S(1)} %get-tuple-element.113), channel_id=1, source_target_pairs={{0,24},{1,7},{2,26},{3,1},{4,28},{5,3},{6,30},{7,5},{8,0},{9,15},{... | collective-permute-start | bytes 221192 | tf_op jit(solution)/shard_map/ppermute | solution.py:860
  81.0 2.2 %collective-permute-done.17.rest_2_ = bf16[96,384]{1,0:T(8,128)(2,1)S(1)} collective-permute-done((bf16[96,384]{1,0:T(8,128)(2,1)S(1)}, bf16[96,384]{1,0:T(8,128)(2,1)S(1)}, u32[]{:S(2)}, u32[]{:S(2)}) %collective-permute-start.17) | collective-permute-done | bytes 73760 | tf_op jit(solution)/shard_map/ppermute | solution.py:860
  83.3 2.1 %collective-permute-start.25 = (bf16[80,384]{1,0:T(8,128)(2,1)S(1)}, bf16[80,384]{1,0:T(8,128)(2,1)S(1)}, u32[]{:S(2)}, u32[]{:S(2)}) collective-permute-start(bf16[80,384]{1,0:T(8,128)(2,1)S(1)} %get-tuple-element.123), channel_id=1, source_target_pairs={{0,4},{1,17},{2,6},{3,19},{4,0},{5,21},{6,2},{7,23},{8,12},{9,25},... | collective-permute-start | bytes 184328 | tf_op jit(solution)/shard_map/ppermute | solution.py:860
  85.4 1.9 %collective-permute-start.26 = (bf16[80,384]{1,0:T(8,128)(2,1)S(1)}, bf16[80,384]{1,0:T(8,128)(2,1)S(1)}, u32[]{:S(2)}, u32[]{:S(2)}) collective-permute-start(bf16[80,384]{1,0:T(8,128)(2,1)S(1)} %get-tuple-element.124), channel_id=1, source_target_pairs={{0,2},{1,9},{2,4},{3,11},{4,6},{5,13},{6,0},{7,15},{8,10},{9,17},{... | collective-permute-start | bytes 184328 | tf_op jit(solution)/shard_map/ppermute | solution.py:860
  87.2 1.4 %collective-permute-start.27 = (bf16[80,384]{1,0:T(8,128)(2,1)S(1)}, bf16[80,384]{1,0:T(8,128)(2,1)S(1)}, u32[]{:S(2)}, u32[]{:S(2)}) collective-permute-start(bf16[80,384]{1,0:T(8,128)(2,1)S(1)} %get-tuple-element.125), channel_id=1, source_target_pairs={{0,6},{1,25},{2,0},{3,27},{4,2},{5,29},{6,4},{7,31},{8,14},{9,1},{... | collective-permute-start | bytes 184328 | tf_op jit(solution)/shard_map/ppermute | solution.py:860
  89.1 1.7 %collective-permute-done.26.rest_2_ = bf16[80,384]{1,0:T(8,128)(2,1)S(1)} collective-permute-done((bf16[80,384]{1,0:T(8,128)(2,1)S(1)}, bf16[80,384]{1,0:T(8,128)(2,1)S(1)}, u32[]{:S(2)}, u32[]{:S(2)}) %collective-permute-start.26) | collective-permute-done | bytes 61472 | tf_op jit(solution)/shard_map/ppermute | solution.py:860
  (46 shorter events, 7.8 us)
Async XLA Ops:
  0.6 1.4 %collective-permute-start = (bf16[2,384]{1,0:T(2,128)(2,1)}, bf16[2,384]{1,0:T(2,128)(2,1)S(1)}, u32[]{:S(2)}, u32[]{:S(2)}) collective-permute-start(bf16[2,384]{1,0:T(2,128)(2,1)} %own.1), channel_id=1, source_target_pairs={{0,1},{1,0},{2,3},{3,2},{4,5},{5,4},{6,7},{7,6},{8,9},{9,8},{10,11... | collective-permute-start | bytes 4616 | tf_op jit(solution)/shard_map/ppermute | solution.py:864
  2.1 0.7 copy-start
  2.8 10.1 %collective-permute-start.3 = (bf16[2,2,384]{2,1,0:T(2,128)(2,1)S(1)}, bf16[2,2,384]{2,1,0:T(2,128)(2,1)S(1)}, u32[]{:S(2)}, u32[]{:S(2)}) collective-permute-start(bf16[2,2,384]{2,1,0:T(2,128)(2,1)S(1)} %join_cores.1.rest_0_), channel_id=1, source_target_pairs={{0,96},{1,97},{2,98},{3,99},{4,100},{5,101},{6,102},{7,103},{8,104... | collective-permute-start | bytes 9224 | tf_op jit(solution)/shard_map/ppermute | solution.py:860
  6.9 6.0 %collective-permute-start.2 = (bf16[2,2,384]{2,1,0:T(2,128)(2,1)S(1)}, bf16[2,2,384]{2,1,0:T(2,128)(2,1)S(1)}, u32[]{:S(2)}, u32[]{:S(2)}) collective-permute-start(bf16[2,2,384]{2,1,0:T(2,128)(2,1)S(1)} %join_cores.1.rest_0_), channel_id=1, source_target_pairs={{0,32},{1,33},{2,34},{3,35},{4,36},{5,37},{6,38},{7,39},{8,40},{9,... | collective-permute-start | bytes 9224 | tf_op jit(solution)/shard_map/ppermute | solution.py:860
  6.9 6.0 %collective-permute-start.1 = (bf16[2,2,384]{2,1,0:T(2,128)(2,1)S(1)}, bf16[2,2,384]{2,1,0:T(2,128)(2,1)S(1)}, u32[]{:S(2)}, u32[]{:S(2)}) collective-permute-start(bf16[2,2,384]{2,1,0:T(2,128)(2,1)S(1)} %join_cores.1.rest_0_), channel_id=1, source_target_pairs={{0,64},{1,65},{2,66},{3,67},{4,68},{5,69},{6,70},{7,71},{8,72},{9,... | collective-permute-start | bytes 9224 | tf_op jit(solution)/shard_map/ppermute | solution.py:860
  12.9 9.0 %collective-permute-start.6 = (bf16[4,2,2,384]{3,2,1,0:T(2,128)(2,1)S(1)}, bf16[4,2,2,384]{3,2,1,0:T(2,128)(2,1)S(1)}, u32[]{:S(2)}, u32[]{:S(2)}) collective-permute-start(bf16[4,2,2,384]{3,2,1,0:T(2,128)(2,1)S(1)} %gather_ring.2._.rest_0_), channel_id=1, source_target_pairs={{0,24},{1,25},{2,26},{3,27},{4,28},{5,29},{6,30},{7,31},{8,0},{9,1... | collective-permute-start | bytes 36872 | tf_op jit(solution)/shard_map/ppermute | solution.py:860
  15.7 6.2 %collective-permute-start.5 = (bf16[4,2,2,384]{3,2,1,0:T(2,128)(2,1)S(1)}, bf16[4,2,2,384]{3,2,1,0:T(2,128)(2,1)S(1)}, u32[]{:S(2)}, u32[]{:S(2)}) collective-permute-start(bf16[4,2,2,384]{3,2,1,0:T(2,128)(2,1)S(1)} %gather_ring.2._.rest_0_), channel_id=1, source_target_pairs={{0,8},{1,9},{2,10},{3,11},{4,12},{5,13},{6,14},{7,15},{8,16},{9,17... | collective-permute-start | bytes 36872 | tf_op jit(solution)/shard_map/ppermute | solution.py:860
  15.7 6.2 %collective-permute-start.4 = (bf16[4,2,2,384]{3,2,1,0:T(2,128)(2,1)S(1)}, bf16[4,2,2,384]{3,2,1,0:T(2,128)(2,1)S(1)}, u32[]{:S(2)}, u32[]{:S(2)}) collective-permute-start(bf16[4,2,2,384]{3,2,1,0:T(2,128)(2,1)S(1)} %gather_ring.2._.rest_0_), channel_id=1, source_target_pairs={{0,16},{1,17},{2,18},{3,19},{4,20},{5,21},{6,22},{7,23},{8,24},{9,... | collective-permute-start | bytes 36872 | tf_op jit(solution)/shard_map/ppermute | solution.py:860
  18.0 9.2 %copy-start.2 = (s32[2]{0:T(128)S(1)}, s32[2]{0:T(128)}, u32[]{:S(2)}) copy-start(s32[2]{0:T(128)} %counts.5) | copy-start | bytes 28
  21.9 8.4 %collective-permute-start.9 = (bf16[4,4,2,2,384]{4,3,2,1,0:T(2,128)(2,1)S(1)}, bf16[4,4,2,2,384]{4,3,2,1,0:T(2,128)(2,1)S(1)}, u32[]{:S(2)}, u32[]{:S(2)}) collective-permute-start(bf16[4,4,2,2,384]{4,3,2,1,0:T(2,128)(2,1)S(1)} %gather_ring.3._.rest_0_), channel_id=1, source_target_pairs={{0,6},{1,7},{2,0},{3,1},{4,2},{5,3},{6,4},{7,5},{8,14},{9,15},{10,... | collective-permute-start | bytes 147464 | tf_op jit(solution)/shard_map/ppermute | solution.py:860
  25.0 5.8 %collective-permute-start.8 = (bf16[4,4,2,2,384]{4,3,2,1,0:T(2,128)(2,1)S(1)}, bf16[4,4,2,2,384]{4,3,2,1,0:T(2,128)(2,1)S(1)}, u32[]{:S(2)}, u32[]{:S(2)}) collective-permute-start(bf16[4,4,2,2,384]{4,3,2,1,0:T(2,128)(2,1)S(1)} %gather_ring.3._.rest_0_), channel_id=1, source_target_pairs={{0,2},{1,3},{2,4},{3,5},{4,6},{5,7},{6,0},{7,1},{8,10},{9,11},{10,... | collective-permute-start | bytes 147464 | tf_op jit(solution)/shard_map/ppermute | solution.py:860
  25.0 5.8 %collective-permute-start.7 = (bf16[4,4,2,2,384]{4,3,2,1,0:T(2,128)(2,1)S(1)}, bf16[4,4,2,2,384]{4,3,2,1,0:T(2,128)(2,1)S(1)}, u32[]{:S(2)}, u32[]{:S(2)}) collective-permute-start(bf16[4,4,2,2,384]{4,3,2,1,0:T(2,128)(2,1)S(1)} %gather_ring.3._.rest_0_), channel_id=1, source_target_pairs={{0,4},{1,5},{2,6},{3,7},{4,0},{5,1},{6,2},{7,3},{8,12},{9,13},{10,... | collective-permute-start | bytes 147464 | tf_op jit(solution)/shard_map/ppermute | solution.py:860
  27.2 3.6 %copy-start.1 = (s32[256]{0:T(256)S(1)}, s32[256]{0:T(256)}, u32[]{:S(2)}) copy-start(s32[256]{0:T(256)} %slot_of.3) | copy-start | bytes 3076
  37.7 10.4 %collective-permute-start.10 = (bf16[4,36,16,384]{3,2,1,0:T(8,128)(2,1)S(1)}, bf16[4,36,16,384]{3,2,1,0:T(8,128)(2,1)S(1)}, u32[]{:S(2)}, u32[]{:S(2)}) collective-permute-start(bf16[4,36,16,384]{3,2,1,0:T(8,128)(2,1)S(1)} %get-tuple-element.89), channel_id=1, source_target_pairs={{0,1},{1,0},{2,3},{3,2},{4,5},{5,4},{6,7},{7,6},{8,9},{9,8},{10,11... | collective-permute-start | bytes 5308424 | tf_op jit(solution)/shard_map/ppermute | solution.py:864
  41.0 7.2 %collective-permute-start.11 = (bf16[4,27,16,384]{3,2,1,0:T(8,128)(2,1)S(1)}, bf16[4,27,16,384]{3,2,1,0:T(8,128)(2,1)S(1)}, u32[]{:S(2)}, u32[]{:S(2)}) collective-permute-start(bf16[4,27,16,384]{3,2,1,0:T(8,128)(2,1)S(1)} %get-tuple-element.95), channel_id=1, source_target_pairs={{0,1},{1,0},{2,3},{3,2},{4,5},{5,4},{6,7},{7,6},{8,9},{9,8},{10,11... | collective-permute-start | bytes 3981320 | tf_op jit(solution)/shard_map/ppermute | solution.py:864
  45.7 2.4 %collective-permute-start.12 = (bf16[4,17,16,384]{3,2,1,0:T(8,128)(2,1)S(1)}, bf16[4,17,16,384]{3,2,1,0:T(8,128)(2,1)S(1)}, u32[]{:S(2)}, u32[]{:S(2)}) collective-permute-start(bf16[4,17,16,384]{3,2,1,0:T(8,128)(2,1)S(1)} %get-tuple-element.105), channel_id=1, source_target_pairs={{0,1},{1,0},{2,3},{3,2},{4,5},{5,4},{6,7},{7,6},{8,9},{9,8},{10,11... | collective-permute-start | bytes 2506760 | tf_op jit(solution)/shard_map/ppermute | solution.py:864
  48.7 12.6 %collective-permute-start.19 = (bf16[56,16,384]{2,1,0:T(8,128)(2,1)S(1)}, bf16[56,16,384]{2,1,0:T(8,128)(2,1)S(1)}, u32[]{:S(2)}, u32[]{:S(2)}) collective-permute-start(bf16[56,16,384]{2,1,0:T(8,128)(2,1)S(1)} %get-tuple-element.115), channel_id=1, source_target_pairs={{0,16},{1,5},{2,18},{3,7},{4,20},{5,1},{6,22},{7,3},{8,24},{9,13},... | collective-permute-start | bytes 2064392 | tf_op jit(solution)/shard_map/ppermute | solution.py:860
  50.1 18.5 %collective-permute-start.20 = (bf16[56,16,384]{2,1,0:T(8,128)(2,1)S(1)}, bf16[56,16,384]{2,1,0:T(8,128)(2,1)S(1)}, u32[]{:S(2)}, u32[]{:S(2)}) collective-permute-start(bf16[56,16,384]{2,1,0:T(8,128)(2,1)S(1)} %get-tuple-element.116), channel_id=1, source_target_pairs={{0,8},{1,3},{2,10},{3,5},{4,12},{5,7},{6,14},{7,1},{8,16},{9,11},{... | collective-permute-start | bytes 2064392 | tf_op jit(solution)/shard_map/ppermute | solution.py:860
  51.9 16.7 %collective-permute-start.21 = (bf16[56,16,384]{2,1,0:T(8,128)(2,1)S(1)}, bf16[56,16,384]{2,1,0:T(8,128)(2,1)S(1)}, u32[]{:S(2)}, u32[]{:S(2)}) collective-permute-start(bf16[56,16,384]{2,1,0:T(8,128)(2,1)S(1)} %get-tuple-element.117), channel_id=1, source_target_pairs={{0,24},{1,7},{2,26},{3,1},{4,28},{5,3},{6,30},{7,5},{8,0},{9,15},{... | collective-permute-start | bytes 2064392 | tf_op jit(solution)/shard_map/ppermute | solution.py:860
  53.3 19.6 %collective-permute-start.13 = (bf16[24,16,384]{2,1,0:T(8,128)(2,1)S(1)}, bf16[24,16,384]{2,1,0:T(8,128)(2,1)S(1)}, u32[]{:S(2)}, u32[]{:S(2)}) collective-permute-start(bf16[24,16,384]{2,1,0:T(8,128)(2,1)S(1)} %get-tuple-element.107), channel_id=1, source_target_pairs={{0,64},{1,65},{2,66},{3,67},{4,68},{5,69},{6,70},{7,71},{8,72},{9,... | collective-permute-start | bytes 884744 | tf_op jit(solution)/shard_map/ppermute | solution.py:860
  55.0 19.7 %collective-permute-start.14 = (bf16[24,16,384]{2,1,0:T(8,128)(2,1)S(1)}, bf16[24,16,384]{2,1,0:T(8,128)(2,1)S(1)}, u32[]{:S(2)}, u32[]{:S(2)}) collective-permute-start(bf16[24,16,384]{2,1,0:T(8,128)(2,1)S(1)} %get-tuple-element.108), channel_id=1, source_target_pairs={{0,32},{1,33},{2,34},{3,35},{4,36},{5,37},{6,38},{7,39},{8,40},{9,... | collective-permute-start | bytes 884744 | tf_op jit(solution)/shard_map/ppermute | solution.py:860
  61.3 13.4 %collective-permute-start.15 = (bf16[24,16,384]{2,1,0:T(8,128)(2,1)S(1)}, bf16[24,16,384]{2,1,0:T(8,128)(2,1)S(1)}, u32[]{:S(2)}, u32[]{:S(2)}) collective-permute-start(bf16[24,16,384]{2,1,0:T(8,128)(2,1)S(1)} %get-tuple-element.109), channel_id=1, source_target_pairs={{0,96},{1,97},{2,98},{3,99},{4,100},{5,101},{6,102},{7,103},{8,104... | collective-permute-start | bytes 884744 | tf_op jit(solution)/shard_map/ppermute | solution.py:860
  69.7 8.6 %collective-permute-start.22 = (bf16[224,384]{1,0:T(8,128)(2,1)S(1)}, bf16[224,384]{1,0:T(8,128)(2,1)S(1)}, u32[]{:S(2)}, u32[]{:S(2)}) collective-permute-start(bf16[224,384]{1,0:T(8,128)(2,1)S(1)} %get-tuple-element.119), channel_id=1, source_target_pairs={{0,64},{1,65},{2,66},{3,67},{4,68},{5,69},{6,70},{7,71},{8,72},{9,... | collective-permute-start | bytes 516104 | tf_op jit(solution)/shard_map/ppermute | solution.py:860
  71.4 9.5 %collective-permute-start.23 = (bf16[224,384]{1,0:T(8,128)(2,1)S(1)}, bf16[224,384]{1,0:T(8,128)(2,1)S(1)}, u32[]{:S(2)}, u32[]{:S(2)}) collective-permute-start(bf16[224,384]{1,0:T(8,128)(2,1)S(1)} %get-tuple-element.120), channel_id=1, source_target_pairs={{0,32},{1,33},{2,34},{3,35},{4,36},{5,37},{6,38},{7,39},{8,40},{9,... | collective-permute-start | bytes 516104 | tf_op jit(solution)/shard_map/ppermute | solution.py:860
  72.9 8.0 %collective-permute-start.24 = (bf16[224,384]{1,0:T(8,128)(2,1)S(1)}, bf16[224,384]{1,0:T(8,128)(2,1)S(1)}, u32[]{:S(2)}, u32[]{:S(2)}) collective-permute-start(bf16[224,384]{1,0:T(8,128)(2,1)S(1)} %get-tuple-element.121), channel_id=1, source_target_pairs={{0,96},{1,97},{2,98},{3,99},{4,100},{5,101},{6,102},{7,103},{8,104... | collective-permute-start | bytes 516104 | tf_op jit(solution)/shard_map/ppermute | solution.py:860
  75.1 5.9 %collective-permute-start.16 = (bf16[96,384]{1,0:T(8,128)(2,1)S(1)}, bf16[96,384]{1,0:T(8,128)(2,1)S(1)}, u32[]{:S(2)}, u32[]{:S(2)}) collective-permute-start(bf16[96,384]{1,0:T(8,128)(2,1)S(1)} %get-tuple-element.111), channel_id=1, source_target_pairs={{0,16},{1,5},{2,18},{3,7},{4,20},{5,1},{6,22},{7,3},{8,24},{9,13},... | collective-permute-start | bytes 221192 | tf_op jit(solution)/shard_map/ppermute | solution.py:860
  77.6 5.6 %collective-permute-start.17 = (bf16[96,384]{1,0:T(8,128)(2,1)S(1)}, bf16[96,384]{1,0:T(8,128)(2,1)S(1)}, u32[]{:S(2)}, u32[]{:S(2)}) collective-permute-start(bf16[96,384]{1,0:T(8,128)(2,1)S(1)} %get-tuple-element.112), channel_id=1, source_target_pairs={{0,8},{1,3},{2,10},{3,5},{4,12},{5,7},{6,14},{7,1},{8,16},{9,11},{... | collective-permute-start | bytes 221192 | tf_op jit(solution)/shard_map/ppermute | solution.py:860
  78.3 4.9 %collective-permute-start.18 = (bf16[96,384]{1,0:T(8,128)(2,1)S(1)}, bf16[96,384]{1,0:T(8,128)(2,1)S(1)}, u32[]{:S(2)}, u32[]{:S(2)}) collective-permute-start(bf16[96,384]{1,0:T(8,128)(2,1)S(1)} %get-tuple-element.113), channel_id=1, source_target_pairs={{0,24},{1,7},{2,26},{3,1},{4,28},{5,3},{6,30},{7,5},{8,0},{9,15},{... | collective-permute-start | bytes 221192 | tf_op jit(solution)/shard_map/ppermute | solution.py:860
  83.3 5.8 %collective-permute-start.25 = (bf16[80,384]{1,0:T(8,128)(2,1)S(1)}, bf16[80,384]{1,0:T(8,128)(2,1)S(1)}, u32[]{:S(2)}, u32[]{:S(2)}) collective-permute-start(bf16[80,384]{1,0:T(8,128)(2,1)S(1)} %get-tuple-element.123), channel_id=1, source_target_pairs={{0,4},{1,17},{2,6},{3,19},{4,0},{5,21},{6,2},{7,23},{8,12},{9,25},... | collective-permute-start | bytes 184328 | tf_op jit(solution)/shard_map/ppermute | solution.py:860
  85.4 5.4 %collective-permute-start.26 = (bf16[80,384]{1,0:T(8,128)(2,1)S(1)}, bf16[80,384]{1,0:T(8,128)(2,1)S(1)}, u32[]{:S(2)}, u32[]{:S(2)}) collective-permute-start(bf16[80,384]{1,0:T(8,128)(2,1)S(1)} %get-tuple-element.124), channel_id=1, source_target_pairs={{0,2},{1,9},{2,4},{3,11},{4,6},{5,13},{6,0},{7,15},{8,10},{9,17},{... | collective-permute-start | bytes 184328 | tf_op jit(solution)/shard_map/ppermute | solution.py:860
  87.2 4.2 %collective-permute-start.27 = (bf16[80,384]{1,0:T(8,128)(2,1)S(1)}, bf16[80,384]{1,0:T(8,128)(2,1)S(1)}, u32[]{:S(2)}, u32[]{:S(2)}) collective-permute-start(bf16[80,384]{1,0:T(8,128)(2,1)S(1)} %get-tuple-element.125), channel_id=1, source_target_pairs={{0,6},{1,25},{2,0},{3,27},{4,2},{5,29},{6,4},{7,31},{8,14},{9,1},{... | collective-permute-start | bytes 184328 | tf_op jit(solution)/shard_map/ppermute | solution.py:860
where the time goes:
time: 92.9 us; the launch traced here: 92.1 us
  starting transfers between devices  43.5 us (47%)
  Pallas kernels  27.9 us (30%)
  waiting for transfers between devices  19.2 us (21%)
    ppermute x24, starting transfers between devices, send_along(): return lax.ppermute(value, AXES, pairs)  42.4 us
    pallas_call x6, Pallas kernels, big_kernel(): pl.pallas_call(kernel, in_specs=[spec for _, spec in operands], out_specs...  24.4 us
    ppermute x24, waiting for transfers between devices, send_along(): return lax.ppermute(value, AXES, pairs)  15.6 us
    ppermute x4, waiting for transfers between devices, swap_cores(): lax.ppermute(value, AXES, [(device, device ^ 1) for device in range(128)])  3.69 us
    pallas_call x9, Pallas kernels, local_kernel(): pl.pallas_call(kernel, in_specs=[IN_VMEM for _ in operands], out_specs=[I...  2.97 us
  transfers between devices with their start and end apart: 28, of which 10 were waited for; matrix products, arithmetic and copies ran while one was open for 0% of the time, Pallas kernels for 21%

commit v1 on v0

--- a/solution.py
+++ b/solution.py
@@ -309,6 +309,19 @@
         [((4, *pieces[0].shape), BF16)],
         [],
         "gather_ring",
+    )[0]
+
+
+def hold_kernel(source, out, sem):
+    copy = pltpu.make_async_copy(source, out, sem.at[0])
+    copy.start()
+    copy.wait()
+
+
+def hold(value):
+    outs = [(value.shape, value.dtype)]
+    return big_kernel(
+        hold_kernel, [(in_hbm(value), IN_HBM)], outs, [], 1000000, 1, "hold"
     )[0]
 
 
@@ -526,7 +539,7 @@
     return jnp.where(cam == iota((SLOTS, 1), 0), 1.0, 0.0)
 
 
-GRAD_COUNTS = {"second": (12, 24), "first_mlp": (12, 15), "first_attention": (0, 17)}
+GRAD_COUNTS = {"second": (12, 24), "first_mlp": (12, 15), "first_attention": (0, 11), "first_patch": (0, 6)}
 
 
 ROWS_D, ROWS_W = (sum(n) for n in zip(*GRAD_COUNTS.values()))
@@ -648,9 +661,9 @@
 
 
 def back_attention_kernel(slot_of, tokens, middle_grad, mixed_grad, gain_a, *rest):
-    names = ("mixed",) + ATTENTION_IN + ("stream", "rows")
+    names = ("mixed",) + ATTENTION_IN + ("stream",)
     held, rest = of_layer(names, rest, 0), rest[len(names) :]
-    keep, send, wide_s = rest
+    keep, send, grad_o, wide_s = rest
     z, x, y, my_core = place_of_device()
     device = z * 32 + x * 8 + y * 2 + my_core
     p = iota((ROWS, 1), 0)
@@ -670,7 +683,7 @@
     spread = mm(jnp.where(learner == wanted, 1.0, 0.0).astype(BF16), tokens[...]).astype(BF16)
     spots = [(ref, a, r) for ref in (keep, send) for a in range(4) for r in range(2)]
     for at, (ref, a, r) in enumerate(spots):
-        ref[a, 15 + r] = spread[at * 16 : at * 16 + 16]
+        ref[a, 9 + r] = spread[at * 16 : at * 16 + 16]
     stream_grad = backward_attention(
         my_core,
         middle_grad[...],
@@ -683,21 +696,38 @@
         0,
         wide_s,
     ).astype(BF16)
+    grad_o[...] = stream_grad
+
+
+def back_patch_kernel(rows, grad, keep, send):
+    my_core = place_of_device()[3]
     for ref, core in ((keep, my_core), (send, 1 - my_core)):
-        tile = mm(turned(pick(order_six(core), PATCH_DIM), held["rows"][...]), stream_grad)
-        emit(tile, [(ref, a, 9 + r) for a in range(4) for r in range(6)])
-
-
-def run_back_attention(slot_of, tokens, middle_grad, mixed_grad, rows, stream, params, store):
-    values = {"qkv": params[1], "stream": stream, "rows": rows}
+        tile = mm(turned(pick(order_six(core), PATCH_DIM), rows[...]), grad[...])
+        emit(tile, [(ref, a, r) for a in range(4) for r in range(6)])
+
+
+def run_back_patch(rows, grad):
+    return big_kernel(
+        back_patch_kernel,
+        [(rows, IN_VMEM), (grad, IN_VMEM)],
+        grad_shapes("first_patch"),
+        [],
+        1000000000,
+        0,
+        "back_patch",
+    )
+
+
+def run_back_attention(slot_of, tokens, middle_grad, mixed_grad, stream, params, store):
+    values = {"qkv": params[1], "stream": stream}
     values.update(store)
-    names = ("mixed",) + ATTENTION_IN + ("stream", "rows")
+    names = ("mixed",) + ATTENTION_IN + ("stream",)
     return big_kernel(
         back_attention_kernel,
         [(slot_of, SCALARS)]
         + [(v, IN_VMEM) for v in (tokens, middle_grad, mixed_grad, params[0])]
         + [(values[k], IN_VMEM) for k in names],
-        grad_shapes("first_attention"),
+        grad_shapes("first_attention") + [((ROWS, D), BF16)],
         [((ROWS, 3 * D), BF16)],
         4000000000,
         0,
@@ -825,8 +855,8 @@
         proj[:, layer] = wide[at_up + 12 : at_up + 15]
         for j in range(3):
             qkv[:, layer, pl.ds(j * D, D)] = wide[at_qkv + j * 3 : at_qkv + j * 3 + 3]
-    patch[...] = wide[48:54]
-    tokens[...] = wide[54:56].astype(BF16)
+    tokens[...] = wide[48:50].astype(BF16)
+    patch[...] = wide[50:56]
 
 
 def last_sum(parts):
@@ -884,7 +914,7 @@
     cotangent,
 ):
     params = (attn_gain, qkv_weight, proj_weight, mlp_gain, up_weight, down_weight)
-    chip = join_cores(cotangent, swap_cores(cotangent))
+    chip = join_cores(hold(cotangent), swap_cores(cotangent))
     ring = exchange([chip] * 4, "zz")
     rows, stream, store_first, params, final_gain = run_embed(
         camera_counts,
@@ -917,18 +947,19 @@
     got_second = swap_cores(send)
     keep_mlp, send, middle_grad, mixed_grad = run_back_mlp(stream_grad, params, store_first)
     got_mlp = swap_cores(send)
-    keep, send = run_back_attention(
+    keep, send, grad = run_back_attention(
         slot_of,
         tokens,
         middle_grad,
         mixed_grad,
-        rows,
         stream,
         params,
         store_first,
     )
     got = swap_cores(send)
-    pieces = add_pairs(keep_second, got_second, keep_mlp, got_mlp, keep, got)
+    keep_patch, send = run_back_patch(rows, grad)
+    got_patch = swap_cores(send)
+    pieces = add_pairs(keep_second, got_second, keep_mlp, got_mlp, keep, got, keep_patch, got_patch)
     wide = exchange(pieces[4:], "xy")
     deep = exchange(pieces[:4], "zz")
     wide = exchange(first_sum("zz", wide), "zz")

time: 92.9 us -> 92.1 us (level)
  waiting for transfers between devices: 19.2 us -> 17.6 us
  Pallas kernels: 27.9 us -> 29 us
    ppermute x4 -> x5, waiting for transfers between devices: 3.69 us -> 1.87 us  [swap_cores(): lax.ppermute(value, AXES, [(device, device ^ 1) for device in range(128)])]
    pallas_call x6 -> x8, Pallas kernels: 24.4 us -> 25.4 us  [big_kernel(): pl.pallas_call(kernel, in_specs=[spec for _, spec in operands], out_specs...]
  transfers between devices with their start and end apart: 28 -> 29, of which waited for: 10 -> 11; matrix products, arithmetic and copies ran while one was open for 0% -> 0% of each run, Pallas kernels for 21% -> 23%
where the time goes in v1:
time: 92.1 us; the launch traced here: 91.3 us
  starting transfers between devices  43.8 us (48%)
  Pallas kernels  29 us (31%)
  waiting for transfers between devices  17.6 us (19%)
    ppermute x24, starting transfers between devices, send_along(): return lax.ppermute(value, AXES, pairs)  42.2 us
    pallas_call x8, Pallas kernels, big_kernel(): pl.pallas_call(kernel, in_specs=[spec for _, spec in operands], out_specs...  25.4 us
    ppermute x24, waiting for transfers between devices, send_along(): return lax.ppermute(value, AXES, pairs)  15.8 us
    pallas_call x9, Pallas kernels, local_kernel(): pl.pallas_call(kernel, in_specs=[IN_VMEM for _ in operands], out_specs=[I...  2.98 us
    ppermute x5, waiting for transfers between devices, swap_cores(): lax.ppermute(value, AXES, [(device, device ^ 1) for device in range(128)])  1.87 us
  transfers between devices with their start and end apart: 29, of which 11 were waited for; matrix products, arithmetic and copies ran while one was open for 0% of the time, Pallas kernels for 23%

profile of v1, /device:TPU:0, one launch (start us, length us, event | category | flops | bytes accessed | tf_op | source)
XLA Modules:
  0.0 91.3 jit_solution(1055876320219260404)
XLA Ops:
  2.1 4.1 %collective-permute-start.3 = (bf16[2,2,384]{2,1,0:T(2,128)(2,1)S(1)}, bf16[2,2,384]{2,1,0:T(2,128)(2,1)S(1)}, u32[]{:S(2)}, u32[]{:S(2)}) collective-permute-start(bf16[2,2,384]{2,1,0:T(2,128)(2,1)S(1)} %join_cores.1.rest_0_), channel_id=1, source_target_pairs={{0,96},{1,97},{2,98},{3,99},{4,100},{5,101},{6,102},{7,103},{8,104... | collective-permute-start | bytes 9224 | tf_op jit(solution)/shard_map/ppermute | solution.py:890
  6.2 1.9 %collective-permute-start.1 = (bf16[2,2,384]{2,1,0:T(2,128)(2,1)S(1)}, bf16[2,2,384]{2,1,0:T(2,128)(2,1)S(1)}, u32[]{:S(2)}, u32[]{:S(2)}) collective-permute-start(bf16[2,2,384]{2,1,0:T(2,128)(2,1)S(1)} %join_cores.1.rest_0_), channel_id=1, source_target_pairs={{0,64},{1,65},{2,66},{3,67},{4,68},{5,69},{6,70},{7,71},{8,72},{9,... | collective-permute-start | bytes 9224 | tf_op jit(solution)/shard_map/ppermute | solution.py:890
  8.1 4.1 %embed_attend.1 = (bf16[256,768]{1,0:T(8,128)(2,1)S(1)}, f32[256,384]{1,0:T(8,128)S(1)}, bf16[256,384]{1,0:T(8,128)(2,1)S(1)}, bf16[256,1152]{1,0:T(8,128)(2,1)S...) custom-call(s32[2]{0:T(128)} %counts.5, ...), custom_call_target="tpu_custom_call" | custom-call | flops 7000000000 | bytes 8000000 | tf_op jit(solution)/shard_map/embed_attend/pallas_call | solution.py:372
  12.2 2.8 %collective-permute-start.6 = (bf16[4,2,2,384]{3,2,1,0:T(2,128)(2,1)S(1)}, bf16[4,2,2,384]{3,2,1,0:T(2,128)(2,1)S(1)}, u32[]{:S(2)}, u32[]{:S(2)}) collective-permute-start(bf16[4,2,2,384]{3,2,1,0:T(2,128)(2,1)S(1)} %gather_ring.2._.rest_0_), channel_id=1, source_target_pairs={{0,24},{1,25},{2,26},{3,27},{4,28},{5,29},{6,30},{7,31},{8,0},{9,1... | collective-permute-start | bytes 36872 | tf_op jit(solution)/shard_map/ppermute | solution.py:890
  15.0 2.3 %collective-permute-start.4 = (bf16[4,2,2,384]{3,2,1,0:T(2,128)(2,1)S(1)}, bf16[4,2,2,384]{3,2,1,0:T(2,128)(2,1)S(1)}, u32[]{:S(2)}, u32[]{:S(2)}) collective-permute-start(bf16[4,2,2,384]{3,2,1,0:T(2,128)(2,1)S(1)} %gather_ring.2._.rest_0_), channel_id=1, source_target_pairs={{0,16},{1,17},{2,18},{3,19},{4,20},{5,21},{6,22},{7,23},{8,24},{9,... | collective-permute-start | bytes 36872 | tf_op jit(solution)/shard_map/ppermute | solution.py:890
  17.3 3.9 %mlp_attend.1 = (f32[256,384]{1,0:T(8,128)S(1)}, bf16[256,384]{1,0:T(8,128)(2,1)S(1)}, bf16[256,1536]{1,0:T(8,128)(2,1)S(1)}, bf16[256,1536]{1,0:T(8,128)(2,1)S(...) custom-call(f32[256,384]{1,0:T(8,128)S(1)} %get-tuple-element.72.mid, ...), custom_call_target="tpu_custom_call" | custom-call | flops 6000000000 | bytes 8000000 | tf_op jit(solution)/shard_map/mlp_attend/pallas_call | solution.py:372
  21.3 3.1 %collective-permute-start.9 = (bf16[4,4,2,2,384]{4,3,2,1,0:T(2,128)(2,1)S(1)}, bf16[4,4,2,2,384]{4,3,2,1,0:T(2,128)(2,1)S(1)}, u32[]{:S(2)}, u32[]{:S(2)}) collective-permute-start(bf16[4,4,2,2,384]{4,3,2,1,0:T(2,128)(2,1)S(1)} %gather_ring.3._.rest_0_), channel_id=1, source_target_pairs={{0,6},{1,7},{2,0},{3,1},{4,2},{5,3},{6,4},{7,5},{8,14},{9,15},{10,... | collective-permute-start | bytes 147464 | tf_op jit(solution)/shard_map/ppermute | solution.py:890
  24.4 2.2 %collective-permute-start.7 = (bf16[4,4,2,2,384]{4,3,2,1,0:T(2,128)(2,1)S(1)}, bf16[4,4,2,2,384]{4,3,2,1,0:T(2,128)(2,1)S(1)}, u32[]{:S(2)}, u32[]{:S(2)}) collective-permute-start(bf16[4,4,2,2,384]{4,3,2,1,0:T(2,128)(2,1)S(1)} %gather_ring.3._.rest_0_), channel_id=1, source_target_pairs={{0,4},{1,5},{2,6},{3,7},{4,0},{5,1},{6,2},{7,3},{8,12},{9,13},{10,... | collective-permute-start | bytes 147464 | tf_op jit(solution)/shard_map/ppermute | solution.py:890
  26.6 3.1 %mlp_pool.1 = (f32[8,384]{1,0:T(8,128)S(1)}, bf16[8,384]{1,0:T(8,128)(2,1)S(1)}, bf16[256,384]{1,0:T(8,128)(2,1)S(1)}, bf16[256,1536]{1,0:T(8,128)(2,1)S(1)}, bf16[256,1536]{1,0:T(8,128)(2,1)S(1)}) custom-call(s32[2]{0:T(128)S(1)} %copy-done.1, f32[256,384]{1,0:T(8,128)S(1)} %get-tuple-element.80.middle.rest_5_, f32[2,384]{1,0:T(2,128)S(1)} %get-tuple-element.74.gain_m, ...), custom_call_target="tpu_custom_call" | custom-call | flops 4000000000 | bytes 8000000 | tf_op jit(solution)/shard_map/mlp_pool/pallas_call | solution.py:372
  30.8 6.2 %back_second.1 = (bf16[4,36,16,384]{3,2,1,0:T(8,128)(2,1)S(1)}, bf16[4,36,16,384]{3,2,1,0:T(8,128)(2,1)S(1)}, f32[256,384]{1,0:T(8,128)S(1)}) custom-call(s32[2]{0:T(128)S(1)} %copy-done.1, f32[2,384]{1,0:T(2,128)S(1)} %take_rows.1.seeds, f32[8,384]{1,0:T(8,128)S(1)} %get-tuple-element.82._.pooled, f32[384]{0:T(512)S(1)} %get-tuple-element.79.rest_4_.final_gain, ...), custom_call_target="tpu_custom_call" | custom-call | flops 8000000000 | bytes 8000000 | tf_op jit(solution)/shard_map/back_second/pallas_call | solution.py:372
  37.1 3.2 %back_first_mlp.1 = (bf16[4,27,16,384]{3,2,1,0:T(8,128)(2,1)S(1)}, bf16[4,27,16,384]{3,2,1,0:T(8,128)(2,1)S(1)}, f32[256,384]{1,0:T(8,128)S(1)}, bf16[256,384]{1,0:T(8,128)(2,1)S(1)}) custom-call(f32[2,384]{1,0:T(2,128)S(1)} %get-tuple-element.74.gain_m, f32[256,384]{1,0:T(8,128)S(1)} %get-tuple-element.93.rest_0_, ...), custom_call_target="tpu_custom_call" | custom-call | flops 5000000000 | bytes 8000000 | tf_op jit(solution)/shard_map/back_first_mlp/pallas_call | solution.py:372
  41.1 3.0 %back_first_attention.1 = (bf16[4,11,16,384]{3,2,1,0:T(8,128)(2,1)S(1)}, bf16[4,11,16,384]{3,2,1,0:T(8,128)(2,1)S(1)}, bf16[256,384]{1,0:T(8,128)(2,1)S(1)}) custom-call(s32[256]{0:T(256)S(1)} %copy-done, bf16[8,384]{1,0:T(8,128)(2,1)S(1)} %get-tuple-element.99.tokens, f32[256,384]{1,0:T(8,128)S(1)} %get-tuple-element.100.middle_grad, ...), custom_call_target="tpu_custom_call" | custom-call | flops 4000000000 | bytes 8000000 | tf_op jit(solution)/shard_map/back_first_attention/pallas_call | solution.py:372
  44.2 1.2 %back_patch.1 = (bf16[4,6,16,384]{3,2,1,0:T(8,128)(2,1)S(1)}, bf16[4,6,16,384]{3,2,1,0:T(8,128)(2,1)S(1)}) custom-call(bf16[256,768]{1,0:T(8,128)(2,1)S(1)} %get-tuple-element.108.rows, bf16[256,384]{1,0:T(8,128)(2,1)S(1)} %get-tuple-element.109.grad), custom_call_target="tpu_custom_call" | custom-call | flops 1000000000 | bytes 8000000 | tf_op jit(solution)/shard_map/back_patch/pallas_call | solution.py:372
  46.0 1.2 %collective-permute-done.13.rest_7_ = bf16[4,6,16,384]{3,2,1,0:T(8,128)(2,1)S(1)} collective-permute-done((bf16[4,6,16,384]{3,2,1,0:T(8,128)(2,1)S(1)}, bf16[4,6,16,384]{3,2,1,0:T(8,128)(2,1)S(1)}, u32[]{:S(2)}, u32[]{:S(2)}) %collective-permute-start.13) | collective-permute-done | bytes 294944 | tf_op jit(solution)/shard_map/ppermute | solution.py:894
  47.8 1.4 %collective-permute-start.20 = (bf16[56,16,384]{2,1,0:T(8,128)(2,1)S(1)}, bf16[56,16,384]{2,1,0:T(8,128)(2,1)S(1)}, u32[]{:S(2)}, u32[]{:S(2)}) collective-permute-start(bf16[56,16,384]{2,1,0:T(8,128)(2,1)S(1)} %get-tuple-element.121), channel_id=1, source_target_pairs={{0,16},{1,5},{2,18},{3,7},{4,20},{5,1},{6,22},{7,3},{8,24},{9,13},... | collective-permute-start | bytes 2064392 | tf_op jit(solution)/shard_map/ppermute | solution.py:890
  49.2 1.8 %collective-permute-start.21 = (bf16[56,16,384]{2,1,0:T(8,128)(2,1)S(1)}, bf16[56,16,384]{2,1,0:T(8,128)(2,1)S(1)}, u32[]{:S(2)}, u32[]{:S(2)}) collective-permute-start(bf16[56,16,384]{2,1,0:T(8,128)(2,1)S(1)} %get-tuple-element.122), channel_id=1, source_target_pairs={{0,8},{1,3},{2,10},{3,5},{4,12},{5,7},{6,14},{7,1},{8,16},{9,11},{... | collective-permute-start | bytes 2064392 | tf_op jit(solution)/shard_map/ppermute | solution.py:890
  51.0 1.4 %collective-permute-start.22 = (bf16[56,16,384]{2,1,0:T(8,128)(2,1)S(1)}, bf16[56,16,384]{2,1,0:T(8,128)(2,1)S(1)}, u32[]{:S(2)}, u32[]{:S(2)}) collective-permute-start(bf16[56,16,384]{2,1,0:T(8,128)(2,1)S(1)} %get-tuple-element.123), channel_id=1, source_target_pairs={{0,24},{1,7},{2,26},{3,1},{4,28},{5,3},{6,30},{7,5},{8,0},{9,15},{... | collective-permute-start | bytes 2064392 | tf_op jit(solution)/shard_map/ppermute | solution.py:890
  52.4 1.7 %collective-permute-start.14 = (bf16[24,16,384]{2,1,0:T(8,128)(2,1)S(1)}, bf16[24,16,384]{2,1,0:T(8,128)(2,1)S(1)}, u32[]{:S(2)}, u32[]{:S(2)}) collective-permute-start(bf16[24,16,384]{2,1,0:T(8,128)(2,1)S(1)} %get-tuple-element.113), channel_id=1, source_target_pairs={{0,64},{1,65},{2,66},{3,67},{4,68},{5,69},{6,70},{7,71},{8,72},{9,... | collective-permute-start | bytes 884744 | tf_op jit(solution)/shard_map/ppermute | solution.py:890
  54.1 1.5 %collective-permute-start.15 = (bf16[24,16,384]{2,1,0:T(8,128)(2,1)S(1)}, bf16[24,16,384]{2,1,0:T(8,128)(2,1)S(1)}, u32[]{:S(2)}, u32[]{:S(2)}) collective-permute-start(bf16[24,16,384]{2,1,0:T(8,128)(2,1)S(1)} %get-tuple-element.114), channel_id=1, source_target_pairs={{0,32},{1,33},{2,34},{3,35},{4,36},{5,37},{6,38},{7,39},{8,40},{9,... | collective-permute-start | bytes 884744 | tf_op jit(solution)/shard_map/ppermute | solution.py:890
  55.5 4.9 %collective-permute-done.20.rest_1_ = bf16[56,16,384]{2,1,0:T(8,128)(2,1)S(1)} collective-permute-done((bf16[56,16,384]{2,1,0:T(8,128)(2,1)S(1)}, bf16[56,16,384]{2,1,0:T(8,128)(2,1)S(1)}, u32[]{:S(2)}, u32[]{:S(2)}) %collective-permute-start.20) | collective-permute-done | bytes 688160 | tf_op jit(solution)/shard_map/ppermute | solution.py:890
  60.4 2.3 %collective-permute-start.16 = (bf16[24,16,384]{2,1,0:T(8,128)(2,1)S(1)}, bf16[24,16,384]{2,1,0:T(8,128)(2,1)S(1)}, u32[]{:S(2)}, u32[]{:S(2)}) collective-permute-start(bf16[24,16,384]{2,1,0:T(8,128)(2,1)S(1)} %get-tuple-element.115), channel_id=1, source_target_pairs={{0,96},{1,97},{2,98},{3,99},{4,100},{5,101},{6,102},{7,103},{8,104... | collective-permute-start | bytes 884744 | tf_op jit(solution)/shard_map/ppermute | solution.py:890
  62.7 5.0 %collective-permute-done.21.rest_2_ = bf16[56,16,384]{2,1,0:T(8,128)(2,1)S(1)} collective-permute-done((bf16[56,16,384]{2,1,0:T(8,128)(2,1)S(1)}, bf16[56,16,384]{2,1,0:T(8,128)(2,1)S(1)}, u32[]{:S(2)}, u32[]{:S(2)}) %collective-permute-start.21) | collective-permute-done | bytes 688160 | tf_op jit(solution)/shard_map/ppermute | solution.py:890
  68.8 1.8 %collective-permute-start.23 = (bf16[224,384]{1,0:T(8,128)(2,1)S(1)}, bf16[224,384]{1,0:T(8,128)(2,1)S(1)}, u32[]{:S(2)}, u32[]{:S(2)}) collective-permute-start(bf16[224,384]{1,0:T(8,128)(2,1)S(1)} %get-tuple-element.125), channel_id=1, source_target_pairs={{0,64},{1,65},{2,66},{3,67},{4,68},{5,69},{6,70},{7,71},{8,72},{9,... | collective-permute-start | bytes 516104 | tf_op jit(solution)/shard_map/ppermute | solution.py:890
  70.6 1.4 %collective-permute-start.24 = (bf16[224,384]{1,0:T(8,128)(2,1)S(1)}, bf16[224,384]{1,0:T(8,128)(2,1)S(1)}, u32[]{:S(2)}, u32[]{:S(2)}) collective-permute-start(bf16[224,384]{1,0:T(8,128)(2,1)S(1)} %get-tuple-element.126), channel_id=1, source_target_pairs={{0,32},{1,33},{2,34},{3,35},{4,36},{5,37},{6,38},{7,39},{8,40},{9,... | collective-permute-start | bytes 516104 | tf_op jit(solution)/shard_map/ppermute | solution.py:890
  72.0 1.8 %collective-permute-start.25 = (bf16[224,384]{1,0:T(8,128)(2,1)S(1)}, bf16[224,384]{1,0:T(8,128)(2,1)S(1)}, u32[]{:S(2)}, u32[]{:S(2)}) collective-permute-start(bf16[224,384]{1,0:T(8,128)(2,1)S(1)} %get-tuple-element.127), channel_id=1, source_target_pairs={{0,96},{1,97},{2,98},{3,99},{4,100},{5,101},{6,102},{7,103},{8,104... | collective-permute-start | bytes 516104 | tf_op jit(solution)/shard_map/ppermute | solution.py:890
  74.2 2.5 %collective-permute-start.17 = (bf16[96,384]{1,0:T(8,128)(2,1)S(1)}, bf16[96,384]{1,0:T(8,128)(2,1)S(1)}, u32[]{:S(2)}, u32[]{:S(2)}) collective-permute-start(bf16[96,384]{1,0:T(8,128)(2,1)S(1)} %get-tuple-element.117), channel_id=1, source_target_pairs={{0,16},{1,5},{2,18},{3,7},{4,20},{5,1},{6,22},{7,3},{8,24},{9,13},... | collective-permute-start | bytes 221192 | tf_op jit(solution)/shard_map/ppermute | solution.py:890
  77.6 2.4 %collective-permute-start.19 = (bf16[96,384]{1,0:T(8,128)(2,1)S(1)}, bf16[96,384]{1,0:T(8,128)(2,1)S(1)}, u32[]{:S(2)}, u32[]{:S(2)}) collective-permute-start(bf16[96,384]{1,0:T(8,128)(2,1)S(1)} %get-tuple-element.119), channel_id=1, source_target_pairs={{0,24},{1,7},{2,26},{3,1},{4,28},{5,3},{6,30},{7,5},{8,0},{9,15},{... | collective-permute-start | bytes 221192 | tf_op jit(solution)/shard_map/ppermute | solution.py:890
  80.3 2.0 %collective-permute-done.18.rest_2_ = bf16[96,384]{1,0:T(8,128)(2,1)S(1)} collective-permute-done((bf16[96,384]{1,0:T(8,128)(2,1)S(1)}, bf16[96,384]{1,0:T(8,128)(2,1)S(1)}, u32[]{:S(2)}, u32[]{:S(2)}) %collective-permute-start.18) | collective-permute-done | bytes 73760 | tf_op jit(solution)/shard_map/ppermute | solution.py:890
  82.4 2.0 %collective-permute-start.26 = (bf16[80,384]{1,0:T(8,128)(2,1)S(1)}, bf16[80,384]{1,0:T(8,128)(2,1)S(1)}, u32[]{:S(2)}, u32[]{:S(2)}) collective-permute-start(bf16[80,384]{1,0:T(8,128)(2,1)S(1)} %get-tuple-element.129), channel_id=1, source_target_pairs={{0,4},{1,17},{2,6},{3,19},{4,0},{5,21},{6,2},{7,23},{8,12},{9,25},... | collective-permute-start | bytes 184328 | tf_op jit(solution)/shard_map/ppermute | solution.py:890
  84.5 1.9 %collective-permute-start.27 = (bf16[80,384]{1,0:T(8,128)(2,1)S(1)}, bf16[80,384]{1,0:T(8,128)(2,1)S(1)}, u32[]{:S(2)}, u32[]{:S(2)}) collective-permute-start(bf16[80,384]{1,0:T(8,128)(2,1)S(1)} %get-tuple-element.130), channel_id=1, source_target_pairs={{0,2},{1,9},{2,4},{3,11},{4,6},{5,13},{6,0},{7,15},{8,10},{9,17},{... | collective-permute-start | bytes 184328 | tf_op jit(solution)/shard_map/ppermute | solution.py:890
  86.4 1.3 %collective-permute-start.28 = (bf16[80,384]{1,0:T(8,128)(2,1)S(1)}, bf16[80,384]{1,0:T(8,128)(2,1)S(1)}, u32[]{:S(2)}, u32[]{:S(2)}) collective-permute-start(bf16[80,384]{1,0:T(8,128)(2,1)S(1)} %get-tuple-element.131), channel_id=1, source_target_pairs={{0,6},{1,25},{2,0},{3,27},{4,2},{5,29},{6,4},{7,31},{8,14},{9,1},{... | collective-permute-start | bytes 184328 | tf_op jit(solution)/shard_map/ppermute | solution.py:890
  88.2 1.7 %collective-permute-done.27.rest_2_ = bf16[80,384]{1,0:T(8,128)(2,1)S(1)} collective-permute-done((bf16[80,384]{1,0:T(8,128)(2,1)S(1)}, bf16[80,384]{1,0:T(8,128)(2,1)S(1)}, u32[]{:S(2)}, u32[]{:S(2)}) %collective-permute-start.27) | collective-permute-done | bytes 61472 | tf_op jit(solution)/shard_map/ppermute | solution.py:890
  (48 shorter events, 9.4 us)
Async XLA Ops:
  0.6 1.4 %collective-permute-start = (bf16[2,384]{1,0:T(2,128)(2,1)}, bf16[2,384]{1,0:T(2,128)(2,1)S(1)}, u32[]{:S(2)}, u32[]{:S(2)}) collective-permute-start(bf16[2,384]{1,0:T(2,128)(2,1)} %source.1), channel_id=1, source_target_pairs={{0,1},{1,0},{2,3},{3,2},{4,5},{5,4},{6,7},{7,6},{8,9},{9,8},{10,11... | collective-permute-start | bytes 4616 | tf_op jit(solution)/shard_map/ppermute | solution.py:894
  2.1 10.1 %collective-permute-start.3 = (bf16[2,2,384]{2,1,0:T(2,128)(2,1)S(1)}, bf16[2,2,384]{2,1,0:T(2,128)(2,1)S(1)}, u32[]{:S(2)}, u32[]{:S(2)}) collective-permute-start(bf16[2,2,384]{2,1,0:T(2,128)(2,1)S(1)} %join_cores.1.rest_0_), channel_id=1, source_target_pairs={{0,96},{1,97},{2,98},{3,99},{4,100},{5,101},{6,102},{7,103},{8,104... | collective-permute-start | bytes 9224 | tf_op jit(solution)/shard_map/ppermute | solution.py:890
  6.2 6.0 %collective-permute-start.2 = (bf16[2,2,384]{2,1,0:T(2,128)(2,1)S(1)}, bf16[2,2,384]{2,1,0:T(2,128)(2,1)S(1)}, u32[]{:S(2)}, u32[]{:S(2)}) collective-permute-start(bf16[2,2,384]{2,1,0:T(2,128)(2,1)S(1)} %join_cores.1.rest_0_), channel_id=1, source_target_pairs={{0,32},{1,33},{2,34},{3,35},{4,36},{5,37},{6,38},{7,39},{8,40},{9,... | collective-permute-start | bytes 9224 | tf_op jit(solution)/shard_map/ppermute | solution.py:890
  6.2 6.0 %collective-permute-start.1 = (bf16[2,2,384]{2,1,0:T(2,128)(2,1)S(1)}, bf16[2,2,384]{2,1,0:T(2,128)(2,1)S(1)}, u32[]{:S(2)}, u32[]{:S(2)}) collective-permute-start(bf16[2,2,384]{2,1,0:T(2,128)(2,1)S(1)} %join_cores.1.rest_0_), channel_id=1, source_target_pairs={{0,64},{1,65},{2,66},{3,67},{4,68},{5,69},{6,70},{7,71},{8,72},{9,... | collective-permute-start | bytes 9224 | tf_op jit(solution)/shard_map/ppermute | solution.py:890
  12.2 9.0 %collective-permute-start.6 = (bf16[4,2,2,384]{3,2,1,0:T(2,128)(2,1)S(1)}, bf16[4,2,2,384]{3,2,1,0:T(2,128)(2,1)S(1)}, u32[]{:S(2)}, u32[]{:S(2)}) collective-permute-start(bf16[4,2,2,384]{3,2,1,0:T(2,128)(2,1)S(1)} %gather_ring.2._.rest_0_), channel_id=1, source_target_pairs={{0,24},{1,25},{2,26},{3,27},{4,28},{5,29},{6,30},{7,31},{8,0},{9,1... | collective-permute-start | bytes 36872 | tf_op jit(solution)/shard_map/ppermute | solution.py:890
  15.0 6.2 %collective-permute-start.5 = (bf16[4,2,2,384]{3,2,1,0:T(2,128)(2,1)S(1)}, bf16[4,2,2,384]{3,2,1,0:T(2,128)(2,1)S(1)}, u32[]{:S(2)}, u32[]{:S(2)}) collective-permute-start(bf16[4,2,2,384]{3,2,1,0:T(2,128)(2,1)S(1)} %gather_ring.2._.rest_0_), channel_id=1, source_target_pairs={{0,8},{1,9},{2,10},{3,11},{4,12},{5,13},{6,14},{7,15},{8,16},{9,17... | collective-permute-start | bytes 36872 | tf_op jit(solution)/shard_map/ppermute | solution.py:890
  15.0 6.2 %collective-permute-start.4 = (bf16[4,2,2,384]{3,2,1,0:T(2,128)(2,1)S(1)}, bf16[4,2,2,384]{3,2,1,0:T(2,128)(2,1)S(1)}, u32[]{:S(2)}, u32[]{:S(2)}) collective-permute-start(bf16[4,2,2,384]{3,2,1,0:T(2,128)(2,1)S(1)} %gather_ring.2._.rest_0_), channel_id=1, source_target_pairs={{0,16},{1,17},{2,18},{3,19},{4,20},{5,21},{6,22},{7,23},{8,24},{9,... | collective-permute-start | bytes 36872 | tf_op jit(solution)/shard_map/ppermute | solution.py:890
  17.3 9.2 %copy-start.1 = (s32[2]{0:T(128)S(1)}, s32[2]{0:T(128)}, u32[]{:S(2)}) copy-start(s32[2]{0:T(128)} %counts.5) | copy-start | bytes 28
  21.3 8.4 %collective-permute-start.9 = (bf16[4,4,2,2,384]{4,3,2,1,0:T(2,128)(2,1)S(1)}, bf16[4,4,2,2,384]{4,3,2,1,0:T(2,128)(2,1)S(1)}, u32[]{:S(2)}, u32[]{:S(2)}) collective-permute-start(bf16[4,4,2,2,384]{4,3,2,1,0:T(2,128)(2,1)S(1)} %gather_ring.3._.rest_0_), channel_id=1, source_target_pairs={{0,6},{1,7},{2,0},{3,1},{4,2},{5,3},{6,4},{7,5},{8,14},{9,15},{10,... | collective-permute-start | bytes 147464 | tf_op jit(solution)/shard_map/ppermute | solution.py:890
  24.4 5.8 %collective-permute-start.8 = (bf16[4,4,2,2,384]{4,3,2,1,0:T(2,128)(2,1)S(1)}, bf16[4,4,2,2,384]{4,3,2,1,0:T(2,128)(2,1)S(1)}, u32[]{:S(2)}, u32[]{:S(2)}) collective-permute-start(bf16[4,4,2,2,384]{4,3,2,1,0:T(2,128)(2,1)S(1)} %gather_ring.3._.rest_0_), channel_id=1, source_target_pairs={{0,2},{1,3},{2,4},{3,5},{4,6},{5,7},{6,0},{7,1},{8,10},{9,11},{10,... | collective-permute-start | bytes 147464 | tf_op jit(solution)/shard_map/ppermute | solution.py:890
  24.4 5.8 %collective-permute-start.7 = (bf16[4,4,2,2,384]{4,3,2,1,0:T(2,128)(2,1)S(1)}, bf16[4,4,2,2,384]{4,3,2,1,0:T(2,128)(2,1)S(1)}, u32[]{:S(2)}, u32[]{:S(2)}) collective-permute-start(bf16[4,4,2,2,384]{4,3,2,1,0:T(2,128)(2,1)S(1)} %gather_ring.3._.rest_0_), channel_id=1, source_target_pairs={{0,4},{1,5},{2,6},{3,7},{4,0},{5,1},{6,2},{7,3},{8,12},{9,13},{10,... | collective-permute-start | bytes 147464 | tf_op jit(solution)/shard_map/ppermute | solution.py:890
  26.6 3.6 %copy-start = (s32[256]{0:T(256)S(1)}, s32[256]{0:T(256)}, u32[]{:S(2)}) copy-start(s32[256]{0:T(256)} %slot_of.3) | copy-start | bytes 3076
  37.0 10.2 %collective-permute-start.10 = (bf16[4,36,16,384]{3,2,1,0:T(8,128)(2,1)S(1)}, bf16[4,36,16,384]{3,2,1,0:T(8,128)(2,1)S(1)}, u32[]{:S(2)}, u32[]{:S(2)}) collective-permute-start(bf16[4,36,16,384]{3,2,1,0:T(8,128)(2,1)S(1)} %get-tuple-element.92), channel_id=1, source_target_pairs={{0,1},{1,0},{2,3},{3,2},{4,5},{5,4},{6,7},{7,6},{8,9},{9,8},{10,11... | collective-permute-start | bytes 5308424 | tf_op jit(solution)/shard_map/ppermute | solution.py:894
  40.3 6.9 %collective-permute-start.11 = (bf16[4,27,16,384]{3,2,1,0:T(8,128)(2,1)S(1)}, bf16[4,27,16,384]{3,2,1,0:T(8,128)(2,1)S(1)}, u32[]{:S(2)}, u32[]{:S(2)}) collective-permute-start(bf16[4,27,16,384]{3,2,1,0:T(8,128)(2,1)S(1)} %get-tuple-element.98), channel_id=1, source_target_pairs={{0,1},{1,0},{2,3},{3,2},{4,5},{5,4},{6,7},{7,6},{8,9},{9,8},{10,11... | collective-permute-start | bytes 3981320 | tf_op jit(solution)/shard_map/ppermute | solution.py:894
  44.1 3.1 %collective-permute-start.12 = (bf16[4,11,16,384]{3,2,1,0:T(8,128)(2,1)S(1)}, bf16[4,11,16,384]{3,2,1,0:T(8,128)(2,1)S(1)}, u32[]{:S(2)}, u32[]{:S(2)}) collective-permute-start(bf16[4,11,16,384]{3,2,1,0:T(8,128)(2,1)S(1)} %get-tuple-element.107), channel_id=1, source_target_pairs={{0,1},{1,0},{2,3},{3,2},{4,5},{5,4},{6,7},{7,6},{8,9},{9,8},{10,11... | collective-permute-start | bytes 1622024 | tf_op jit(solution)/shard_map/ppermute | solution.py:894
  45.4 1.8 %collective-permute-start.13 = (bf16[4,6,16,384]{3,2,1,0:T(8,128)(2,1)S(1)}, bf16[4,6,16,384]{3,2,1,0:T(8,128)(2,1)S(1)}, u32[]{:S(2)}, u32[]{:S(2)}) collective-permute-start(bf16[4,6,16,384]{3,2,1,0:T(8,128)(2,1)S(1)} %get-tuple-element.111), channel_id=1, source_target_pairs={{0,1},{1,0},{2,3},{3,2},{4,5},{5,4},{6,7},{7,6},{8,9},{9,8},{10,11... | collective-permute-start | bytes 884744 | tf_op jit(solution)/shard_map/ppermute | solution.py:894
  47.8 12.6 %collective-permute-start.20 = (bf16[56,16,384]{2,1,0:T(8,128)(2,1)S(1)}, bf16[56,16,384]{2,1,0:T(8,128)(2,1)S(1)}, u32[]{:S(2)}, u32[]{:S(2)}) collective-permute-start(bf16[56,16,384]{2,1,0:T(8,128)(2,1)S(1)} %get-tuple-element.121), channel_id=1, source_target_pairs={{0,16},{1,5},{2,18},{3,7},{4,20},{5,1},{6,22},{7,3},{8,24},{9,13},... | collective-permute-start | bytes 2064392 | tf_op jit(solution)/shard_map/ppermute | solution.py:890
  49.2 18.5 %collective-permute-start.21 = (bf16[56,16,384]{2,1,0:T(8,128)(2,1)S(1)}, bf16[56,16,384]{2,1,0:T(8,128)(2,1)S(1)}, u32[]{:S(2)}, u32[]{:S(2)}) collective-permute-start(bf16[56,16,384]{2,1,0:T(8,128)(2,1)S(1)} %get-tuple-element.122), channel_id=1, source_target_pairs={{0,8},{1,3},{2,10},{3,5},{4,12},{5,7},{6,14},{7,1},{8,16},{9,11},{... | collective-permute-start | bytes 2064392 | tf_op jit(solution)/shard_map/ppermute | solution.py:890
  51.0 16.7 %collective-permute-start.22 = (bf16[56,16,384]{2,1,0:T(8,128)(2,1)S(1)}, bf16[56,16,384]{2,1,0:T(8,128)(2,1)S(1)}, u32[]{:S(2)}, u32[]{:S(2)}) collective-permute-start(bf16[56,16,384]{2,1,0:T(8,128)(2,1)S(1)} %get-tuple-element.123), channel_id=1, source_target_pairs={{0,24},{1,7},{2,26},{3,1},{4,28},{5,3},{6,30},{7,5},{8,0},{9,15},{... | collective-permute-start | bytes 2064392 | tf_op jit(solution)/shard_map/ppermute | solution.py:890
  52.4 19.6 %collective-permute-start.14 = (bf16[24,16,384]{2,1,0:T(8,128)(2,1)S(1)}, bf16[24,16,384]{2,1,0:T(8,128)(2,1)S(1)}, u32[]{:S(2)}, u32[]{:S(2)}) collective-permute-start(bf16[24,16,384]{2,1,0:T(8,128)(2,1)S(1)} %get-tuple-element.113), channel_id=1, source_target_pairs={{0,64},{1,65},{2,66},{3,67},{4,68},{5,69},{6,70},{7,71},{8,72},{9,... | collective-permute-start | bytes 884744 | tf_op jit(solution)/shard_map/ppermute | solution.py:890
  54.1 19.7 %collective-permute-start.15 = (bf16[24,16,384]{2,1,0:T(8,128)(2,1)S(1)}, bf16[24,16,384]{2,1,0:T(8,128)(2,1)S(1)}, u32[]{:S(2)}, u32[]{:S(2)}) collective-permute-start(bf16[24,16,384]{2,1,0:T(8,128)(2,1)S(1)} %get-tuple-element.114), channel_id=1, source_target_pairs={{0,32},{1,33},{2,34},{3,35},{4,36},{5,37},{6,38},{7,39},{8,40},{9,... | collective-permute-start | bytes 884744 | tf_op jit(solution)/shard_map/ppermute | solution.py:890
  60.4 13.4 %collective-permute-start.16 = (bf16[24,16,384]{2,1,0:T(8,128)(2,1)S(1)}, bf16[24,16,384]{2,1,0:T(8,128)(2,1)S(1)}, u32[]{:S(2)}, u32[]{:S(2)}) collective-permute-start(bf16[24,16,384]{2,1,0:T(8,128)(2,1)S(1)} %get-tuple-element.115), channel_id=1, source_target_pairs={{0,96},{1,97},{2,98},{3,99},{4,100},{5,101},{6,102},{7,103},{8,104... | collective-permute-start | bytes 884744 | tf_op jit(solution)/shard_map/ppermute | solution.py:890
  68.8 8.8 %collective-permute-start.23 = (bf16[224,384]{1,0:T(8,128)(2,1)S(1)}, bf16[224,384]{1,0:T(8,128)(2,1)S(1)}, u32[]{:S(2)}, u32[]{:S(2)}) collective-permute-start(bf16[224,384]{1,0:T(8,128)(2,1)S(1)} %get-tuple-element.125), channel_id=1, source_target_pairs={{0,64},{1,65},{2,66},{3,67},{4,68},{5,69},{6,70},{7,71},{8,72},{9,... | collective-permute-start | bytes 516104 | tf_op jit(solution)/shard_map/ppermute | solution.py:890
  70.6 9.7 %collective-permute-start.24 = (bf16[224,384]{1,0:T(8,128)(2,1)S(1)}, bf16[224,384]{1,0:T(8,128)(2,1)S(1)}, u32[]{:S(2)}, u32[]{:S(2)}) collective-permute-start(bf16[224,384]{1,0:T(8,128)(2,1)S(1)} %get-tuple-element.126), channel_id=1, source_target_pairs={{0,32},{1,33},{2,34},{3,35},{4,36},{5,37},{6,38},{7,39},{8,40},{9,... | collective-permute-start | bytes 516104 | tf_op jit(solution)/shard_map/ppermute | solution.py:890
  72.0 8.2 %collective-permute-start.25 = (bf16[224,384]{1,0:T(8,128)(2,1)S(1)}, bf16[224,384]{1,0:T(8,128)(2,1)S(1)}, u32[]{:S(2)}, u32[]{:S(2)}) collective-permute-start(bf16[224,384]{1,0:T(8,128)(2,1)S(1)} %get-tuple-element.127), channel_id=1, source_target_pairs={{0,96},{1,97},{2,98},{3,99},{4,100},{5,101},{6,102},{7,103},{8,104... | collective-permute-start | bytes 516104 | tf_op jit(solution)/shard_map/ppermute | solution.py:890
  74.2 6.1 %collective-permute-start.17 = (bf16[96,384]{1,0:T(8,128)(2,1)S(1)}, bf16[96,384]{1,0:T(8,128)(2,1)S(1)}, u32[]{:S(2)}, u32[]{:S(2)}) collective-permute-start(bf16[96,384]{1,0:T(8,128)(2,1)S(1)} %get-tuple-element.117), channel_id=1, source_target_pairs={{0,16},{1,5},{2,18},{3,7},{4,20},{5,1},{6,22},{7,3},{8,24},{9,13},... | collective-permute-start | bytes 221192 | tf_op jit(solution)/shard_map/ppermute | solution.py:890
  76.8 5.6 %collective-permute-start.18 = (bf16[96,384]{1,0:T(8,128)(2,1)S(1)}, bf16[96,384]{1,0:T(8,128)(2,1)S(1)}, u32[]{:S(2)}, u32[]{:S(2)}) collective-permute-start(bf16[96,384]{1,0:T(8,128)(2,1)S(1)} %get-tuple-element.118), channel_id=1, source_target_pairs={{0,8},{1,3},{2,10},{3,5},{4,12},{5,7},{6,14},{7,1},{8,16},{9,11},{... | collective-permute-start | bytes 221192 | tf_op jit(solution)/shard_map/ppermute | solution.py:890
  77.6 4.7 %collective-permute-start.19 = (bf16[96,384]{1,0:T(8,128)(2,1)S(1)}, bf16[96,384]{1,0:T(8,128)(2,1)S(1)}, u32[]{:S(2)}, u32[]{:S(2)}) collective-permute-start(bf16[96,384]{1,0:T(8,128)(2,1)S(1)} %get-tuple-element.119), channel_id=1, source_target_pairs={{0,24},{1,7},{2,26},{3,1},{4,28},{5,3},{6,30},{7,5},{8,0},{9,15},{... | collective-permute-start | bytes 221192 | tf_op jit(solution)/shard_map/ppermute | solution.py:890
  82.4 5.8 %collective-permute-start.26 = (bf16[80,384]{1,0:T(8,128)(2,1)S(1)}, bf16[80,384]{1,0:T(8,128)(2,1)S(1)}, u32[]{:S(2)}, u32[]{:S(2)}) collective-permute-start(bf16[80,384]{1,0:T(8,128)(2,1)S(1)} %get-tuple-element.129), channel_id=1, source_target_pairs={{0,4},{1,17},{2,6},{3,19},{4,0},{5,21},{6,2},{7,23},{8,12},{9,25},... | collective-permute-start | bytes 184328 | tf_op jit(solution)/shard_map/ppermute | solution.py:890
  84.5 5.4 %collective-permute-start.27 = (bf16[80,384]{1,0:T(8,128)(2,1)S(1)}, bf16[80,384]{1,0:T(8,128)(2,1)S(1)}, u32[]{:S(2)}, u32[]{:S(2)}) collective-permute-start(bf16[80,384]{1,0:T(8,128)(2,1)S(1)} %get-tuple-element.130), channel_id=1, source_target_pairs={{0,2},{1,9},{2,4},{3,11},{4,6},{5,13},{6,0},{7,15},{8,10},{9,17},{... | collective-permute-start | bytes 184328 | tf_op jit(solution)/shard_map/ppermute | solution.py:890
  86.4 4.2 %collective-permute-start.28 = (bf16[80,384]{1,0:T(8,128)(2,1)S(1)}, bf16[80,384]{1,0:T(8,128)(2,1)S(1)}, u32[]{:S(2)}, u32[]{:S(2)}) collective-permute-start(bf16[80,384]{1,0:T(8,128)(2,1)S(1)} %get-tuple-element.131), channel_id=1, source_target_pairs={{0,6},{1,25},{2,0},{3,27},{4,2},{5,29},{6,4},{7,31},{8,14},{9,1},{... | collective-permute-start | bytes 184328 | tf_op jit(solution)/shard_map/ppermute | solution.py:890

commit v2 on v1

--- a/solution.py
+++ b/solution.py
@@ -339,7 +339,7 @@
     pieces, (out, held_s) = rest[:4], rest[4:]
     z, x, y, my_core = place_of_device()
     for step, piece in zip((0, *STEPS), pieces, strict=True):
-        held_s[lax.bitwise_and(y - step, 3)] = piece[...].astype(F32)
+        held_s[lax.bitwise_and(y - step, 3)] = piece[...]
     device = z * 32 + x * 8 + y * 2 + my_core
     row = iota((2, 1), 0)
     taken = []
@@ -350,7 +350,7 @@
             lax.bitwise_and(lax.shift_right_logical(slot, 4), 3),
             lax.shift_right_logical(slot, 6),
             lax.bitwise_and(lax.shift_right_logical(slot, 1), 1),
-        ]
+        ].astype(F32)
         chosen = row == lax.bitwise_and(slot, 1)
         taken.append(jnp.sum(jnp.where(chosen, pair, 0.0), axis=0, keepdims=True))
     out[...] = jnp.where(row == 0, taken[0], taken[1])
@@ -362,7 +362,7 @@
         in_specs=[SCALARS, ANY_SPEC] + [IN_VMEM] * 4,
         out_specs=[IN_VMEM],
         out_shape=shapes_of([((2, D), F32)]),
-        scratch_shapes=[pltpu.VMEM((4, 4, 4, 2, 2, D), F32)],
+        scratch_shapes=[pltpu.VMEM((4, 4, 4, 2, 2, D), BF16)],
         compiler_params=pltpu.CompilerParams(vmem_limit_bytes=SMALL_VMEM_BYTES),
         name="take_rows",
     )(slot_of, after, *pieces)[0]
@@ -788,19 +788,17 @@
 
 
 def first_sum_kernel(axes, *rest):
-    parts, outs, (total_s, turn_s) = rest[:4], rest[4:8], rest[8:]
+    parts, outs, total_s = rest[:4], rest[4:8], rest[8]
     count = parts[0].shape[0]
     total = sum_of(parts).reshape(count * 16, D)
     for lanes in range(3):
         total_s[lanes] = total[:, lanes * 128 : lanes * 128 + 128]
-    for b in range(16):
-        for lanes in range(3):
-            turn_s[b // 4, pl.ds(b % 4 * count, count), pl.ds(lanes * 128, 128)] = total_s[
-                lanes, pl.ds(b, count, 16)
-            ]
     along = place_on(axes)
     for step in range(4):
-        outs[step][...] = turn_s[lax.bitwise_and(along + step, 3)].astype(BF16)
+        second = lax.bitwise_and(along + step, 3)
+        for lanes in range(3):
+            rows = [total_s[lanes, pl.ds(second * 4 + third, count, 16)] for third in range(4)]
+            outs[step][:, pl.ds(lanes * 128, 128)] = jnp.concatenate(rows, axis=0).astype(BF16)
 
 
 def first_sum(axes, parts):
@@ -809,7 +807,7 @@
         partial(first_sum_kernel, axes),
         parts,
         [((4 * count, D), BF16)] * 4,
-        [pltpu.VMEM((3, count * 16, 128), F32), pltpu.VMEM((4, 4 * count, D), F32)],
+        [pltpu.VMEM((3, count * 16, 128), F32)],
         "first_sum",
     )
 

time: 92.1 us -> 92 us (level)
  no operation moved by 1% of the time
where the time goes in v2:
time: 92 us; the launch traced here: 91.1 us
  starting transfers between devices  43.8 us (48%)
  Pallas kernels  28.8 us (31%)
  waiting for transfers between devices  17.7 us (19%)
    ppermute x24, starting transfers between devices, send_along(): return lax.ppermute(value, AXES, pairs)  42.1 us
    pallas_call x8, Pallas kernels, big_kernel(): pl.pallas_call(kernel, in_specs=[spec for _, spec in operands], out_specs...  25.4 us
    ppermute x24, waiting for transfers between devices, send_along(): return lax.ppermute(value, AXES, pairs)  15.8 us
    pallas_call x9, Pallas kernels, local_kernel(): pl.pallas_call(kernel, in_specs=[IN_VMEM for _ in operands], out_specs=[I...  2.86 us
    ppermute x5, waiting for transfers between devices, swap_cores(): lax.ppermute(value, AXES, [(device, device ^ 1) for device in range(128)])  1.87 us
  transfers between devices with their start and end apart: 29, of which 11 were waited for; matrix products, arithmetic and copies ran while one was open for 0% of the time, Pallas kernels for 23%

profile of v2, /device:TPU:0, one launch (start us, length us, event | category | flops | bytes accessed | tf_op | source)
XLA Modules:
  0.0 91.1 jit_solution(12723747363071264463)
XLA Ops:
  2.1 4.1 %collective-permute-start.3 = (bf16[2,2,384]{2,1,0:T(2,128)(2,1)S(1)}, bf16[2,2,384]{2,1,0:T(2,128)(2,1)S(1)}, u32[]{:S(2)}, u32[]{:S(2)}) collective-permute-start(bf16[2,2,384]{2,1,0:T(2,128)(2,1)S(1)} %join_cores.1.rest_0_), channel_id=1, source_target_pairs={{0,96},{1,97},{2,98},{3,99},{4,100},{5,101},{6,102},{7,103},{8,104... | collective-permute-start | bytes 9224 | tf_op jit(solution)/shard_map/ppermute | solution.py:888
  6.2 1.9 %collective-permute-start.1 = (bf16[2,2,384]{2,1,0:T(2,128)(2,1)S(1)}, bf16[2,2,384]{2,1,0:T(2,128)(2,1)S(1)}, u32[]{:S(2)}, u32[]{:S(2)}) collective-permute-start(bf16[2,2,384]{2,1,0:T(2,128)(2,1)S(1)} %join_cores.1.rest_0_), channel_id=1, source_target_pairs={{0,64},{1,65},{2,66},{3,67},{4,68},{5,69},{6,70},{7,71},{8,72},{9,... | collective-permute-start | bytes 9224 | tf_op jit(solution)/shard_map/ppermute | solution.py:888
  8.1 4.1 %embed_attend.1 = (bf16[256,768]{1,0:T(8,128)(2,1)S(1)}, f32[256,384]{1,0:T(8,128)S(1)}, bf16[256,384]{1,0:T(8,128)(2,1)S(1)}, bf16[256,1152]{1,0:T(8,128)(2,1)S...) custom-call(s32[2]{0:T(128)} %counts.5, ...), custom_call_target="tpu_custom_call" | custom-call | flops 7000000000 | bytes 8000000 | tf_op jit(solution)/shard_map/embed_attend/pallas_call | solution.py:372
  12.2 2.8 %collective-permute-start.6 = (bf16[4,2,2,384]{3,2,1,0:T(2,128)(2,1)S(1)}, bf16[4,2,2,384]{3,2,1,0:T(2,128)(2,1)S(1)}, u32[]{:S(2)}, u32[]{:S(2)}) collective-permute-start(bf16[4,2,2,384]{3,2,1,0:T(2,128)(2,1)S(1)} %gather_ring.2._.rest_0_), channel_id=1, source_target_pairs={{0,24},{1,25},{2,26},{3,27},{4,28},{5,29},{6,30},{7,31},{8,0},{9,1... | collective-permute-start | bytes 36872 | tf_op jit(solution)/shard_map/ppermute | solution.py:888
  15.0 2.3 %collective-permute-start.4 = (bf16[4,2,2,384]{3,2,1,0:T(2,128)(2,1)S(1)}, bf16[4,2,2,384]{3,2,1,0:T(2,128)(2,1)S(1)}, u32[]{:S(2)}, u32[]{:S(2)}) collective-permute-start(bf16[4,2,2,384]{3,2,1,0:T(2,128)(2,1)S(1)} %gather_ring.2._.rest_0_), channel_id=1, source_target_pairs={{0,16},{1,17},{2,18},{3,19},{4,20},{5,21},{6,22},{7,23},{8,24},{9,... | collective-permute-start | bytes 36872 | tf_op jit(solution)/shard_map/ppermute | solution.py:888
  17.3 3.9 %mlp_attend.1 = (f32[256,384]{1,0:T(8,128)S(1)}, bf16[256,384]{1,0:T(8,128)(2,1)S(1)}, bf16[256,1536]{1,0:T(8,128)(2,1)S(1)}, bf16[256,1536]{1,0:T(8,128)(2,1)S(...) custom-call(f32[256,384]{1,0:T(8,128)S(1)} %get-tuple-element.72.mid, ...), custom_call_target="tpu_custom_call" | custom-call | flops 6000000000 | bytes 8000000 | tf_op jit(solution)/shard_map/mlp_attend/pallas_call | solution.py:372
  21.3 3.1 %collective-permute-start.9 = (bf16[4,4,2,2,384]{4,3,2,1,0:T(2,128)(2,1)S(1)}, bf16[4,4,2,2,384]{4,3,2,1,0:T(2,128)(2,1)S(1)}, u32[]{:S(2)}, u32[]{:S(2)}) collective-permute-start(bf16[4,4,2,2,384]{4,3,2,1,0:T(2,128)(2,1)S(1)} %gather_ring.3._.rest_0_), channel_id=1, source_target_pairs={{0,6},{1,7},{2,0},{3,1},{4,2},{5,3},{6,4},{7,5},{8,14},{9,15},{10,... | collective-permute-start | bytes 147464 | tf_op jit(solution)/shard_map/ppermute | solution.py:888
  24.4 2.2 %collective-permute-start.7 = (bf16[4,4,2,2,384]{4,3,2,1,0:T(2,128)(2,1)S(1)}, bf16[4,4,2,2,384]{4,3,2,1,0:T(2,128)(2,1)S(1)}, u32[]{:S(2)}, u32[]{:S(2)}) collective-permute-start(bf16[4,4,2,2,384]{4,3,2,1,0:T(2,128)(2,1)S(1)} %gather_ring.3._.rest_0_), channel_id=1, source_target_pairs={{0,4},{1,5},{2,6},{3,7},{4,0},{5,1},{6,2},{7,3},{8,12},{9,13},{10,... | collective-permute-start | bytes 147464 | tf_op jit(solution)/shard_map/ppermute | solution.py:888
  26.6 3.1 %mlp_pool.1 = (f32[8,384]{1,0:T(8,128)S(1)}, bf16[8,384]{1,0:T(8,128)(2,1)S(1)}, bf16[256,384]{1,0:T(8,128)(2,1)S(1)}, bf16[256,1536]{1,0:T(8,128)(2,1)S(1)}, bf16[256,1536]{1,0:T(8,128)(2,1)S(1)}) custom-call(s32[2]{0:T(128)S(1)} %copy-done.1, f32[256,384]{1,0:T(8,128)S(1)} %get-tuple-element.80.middle.rest_5_, f32[2,384]{1,0:T(2,128)S(1)} %get-tuple-element.74.gain_m, ...), custom_call_target="tpu_custom_call" | custom-call | flops 4000000000 | bytes 8000000 | tf_op jit(solution)/shard_map/mlp_pool/pallas_call | solution.py:372
  30.8 6.2 %back_second.1 = (bf16[4,36,16,384]{3,2,1,0:T(8,128)(2,1)S(1)}, bf16[4,36,16,384]{3,2,1,0:T(8,128)(2,1)S(1)}, f32[256,384]{1,0:T(8,128)S(1)}) custom-call(s32[2]{0:T(128)S(1)} %copy-done.1, f32[2,384]{1,0:T(2,128)S(1)} %take_rows.1.seeds, f32[8,384]{1,0:T(8,128)S(1)} %get-tuple-element.82._.pooled, f32[384]{0:T(512)S(1)} %get-tuple-element.79.rest_4_.final_gain, ...), custom_call_target="tpu_custom_call" | custom-call | flops 8000000000 | bytes 8000000 | tf_op jit(solution)/shard_map/back_second/pallas_call | solution.py:372
  37.1 3.2 %back_first_mlp.1 = (bf16[4,27,16,384]{3,2,1,0:T(8,128)(2,1)S(1)}, bf16[4,27,16,384]{3,2,1,0:T(8,128)(2,1)S(1)}, f32[256,384]{1,0:T(8,128)S(1)}, bf16[256,384]{1,0:T(8,128)(2,1)S(1)}) custom-call(f32[2,384]{1,0:T(2,128)S(1)} %get-tuple-element.74.gain_m, f32[256,384]{1,0:T(8,128)S(1)} %get-tuple-element.93.rest_0_, ...), custom_call_target="tpu_custom_call" | custom-call | flops 5000000000 | bytes 8000000 | tf_op jit(solution)/shard_map/back_first_mlp/pallas_call | solution.py:372
  41.1 3.0 %back_first_attention.1 = (bf16[4,11,16,384]{3,2,1,0:T(8,128)(2,1)S(1)}, bf16[4,11,16,384]{3,2,1,0:T(8,128)(2,1)S(1)}, bf16[256,384]{1,0:T(8,128)(2,1)S(1)}) custom-call(s32[256]{0:T(256)S(1)} %copy-done, bf16[8,384]{1,0:T(8,128)(2,1)S(1)} %get-tuple-element.99.tokens, f32[256,384]{1,0:T(8,128)S(1)} %get-tuple-element.100.middle_grad, ...), custom_call_target="tpu_custom_call" | custom-call | flops 4000000000 | bytes 8000000 | tf_op jit(solution)/shard_map/back_first_attention/pallas_call | solution.py:372
  44.2 1.2 %back_patch.1 = (bf16[4,6,16,384]{3,2,1,0:T(8,128)(2,1)S(1)}, bf16[4,6,16,384]{3,2,1,0:T(8,128)(2,1)S(1)}) custom-call(bf16[256,768]{1,0:T(8,128)(2,1)S(1)} %get-tuple-element.108.rows, bf16[256,384]{1,0:T(8,128)(2,1)S(1)} %get-tuple-element.109.grad), custom_call_target="tpu_custom_call" | custom-call | flops 1000000000 | bytes 8000000 | tf_op jit(solution)/shard_map/back_patch/pallas_call | solution.py:372
  46.0 1.2 %collective-permute-done.13.rest_7_ = bf16[4,6,16,384]{3,2,1,0:T(8,128)(2,1)S(1)} collective-permute-done((bf16[4,6,16,384]{3,2,1,0:T(8,128)(2,1)S(1)}, bf16[4,6,16,384]{3,2,1,0:T(8,128)(2,1)S(1)}, u32[]{:S(2)}, u32[]{:S(2)}) %collective-permute-start.13) | collective-permute-done | bytes 294944 | tf_op jit(solution)/shard_map/ppermute | solution.py:892
  47.8 1.4 %collective-permute-start.20 = (bf16[56,16,384]{2,1,0:T(8,128)(2,1)S(1)}, bf16[56,16,384]{2,1,0:T(8,128)(2,1)S(1)}, u32[]{:S(2)}, u32[]{:S(2)}) collective-permute-start(bf16[56,16,384]{2,1,0:T(8,128)(2,1)S(1)} %get-tuple-element.121), channel_id=1, source_target_pairs={{0,16},{1,5},{2,18},{3,7},{4,20},{5,1},{6,22},{7,3},{8,24},{9,13},... | collective-permute-start | bytes 2064392 | tf_op jit(solution)/shard_map/ppermute | solution.py:888
  49.2 1.8 %collective-permute-start.21 = (bf16[56,16,384]{2,1,0:T(8,128)(2,1)S(1)}, bf16[56,16,384]{2,1,0:T(8,128)(2,1)S(1)}, u32[]{:S(2)}, u32[]{:S(2)}) collective-permute-start(bf16[56,16,384]{2,1,0:T(8,128)(2,1)S(1)} %get-tuple-element.122), channel_id=1, source_target_pairs={{0,8},{1,3},{2,10},{3,5},{4,12},{5,7},{6,14},{7,1},{8,16},{9,11},{... | collective-permute-start | bytes 2064392 | tf_op jit(solution)/shard_map/ppermute | solution.py:888
  51.0 1.4 %collective-permute-start.22 = (bf16[56,16,384]{2,1,0:T(8,128)(2,1)S(1)}, bf16[56,16,384]{2,1,0:T(8,128)(2,1)S(1)}, u32[]{:S(2)}, u32[]{:S(2)}) collective-permute-start(bf16[56,16,384]{2,1,0:T(8,128)(2,1)S(1)} %get-tuple-element.123), channel_id=1, source_target_pairs={{0,24},{1,7},{2,26},{3,1},{4,28},{5,3},{6,30},{7,5},{8,0},{9,15},{... | collective-permute-start | bytes 2064392 | tf_op jit(solution)/shard_map/ppermute | solution.py:888
  52.4 1.7 %collective-permute-start.14 = (bf16[24,16,384]{2,1,0:T(8,128)(2,1)S(1)}, bf16[24,16,384]{2,1,0:T(8,128)(2,1)S(1)}, u32[]{:S(2)}, u32[]{:S(2)}) collective-permute-start(bf16[24,16,384]{2,1,0:T(8,128)(2,1)S(1)} %get-tuple-element.113), channel_id=1, source_target_pairs={{0,64},{1,65},{2,66},{3,67},{4,68},{5,69},{6,70},{7,71},{8,72},{9,... | collective-permute-start | bytes 884744 | tf_op jit(solution)/shard_map/ppermute | solution.py:888
  54.1 1.4 %collective-permute-start.15 = (bf16[24,16,384]{2,1,0:T(8,128)(2,1)S(1)}, bf16[24,16,384]{2,1,0:T(8,128)(2,1)S(1)}, u32[]{:S(2)}, u32[]{:S(2)}) collective-permute-start(bf16[24,16,384]{2,1,0:T(8,128)(2,1)S(1)} %get-tuple-element.114), channel_id=1, source_target_pairs={{0,32},{1,33},{2,34},{3,35},{4,36},{5,37},{6,38},{7,39},{8,40},{9,... | collective-permute-start | bytes 884744 | tf_op jit(solution)/shard_map/ppermute | solution.py:888
  55.5 4.9 %collective-permute-done.20.rest_1_ = bf16[56,16,384]{2,1,0:T(8,128)(2,1)S(1)} collective-permute-done((bf16[56,16,384]{2,1,0:T(8,128)(2,1)S(1)}, bf16[56,16,384]{2,1,0:T(8,128)(2,1)S(1)}, u32[]{:S(2)}, u32[]{:S(2)}) %collective-permute-start.20) | collective-permute-done | bytes 688160 | tf_op jit(solution)/shard_map/ppermute | solution.py:888
  60.4 2.3 %collective-permute-start.16 = (bf16[24,16,384]{2,1,0:T(8,128)(2,1)S(1)}, bf16[24,16,384]{2,1,0:T(8,128)(2,1)S(1)}, u32[]{:S(2)}, u32[]{:S(2)}) collective-permute-start(bf16[24,16,384]{2,1,0:T(8,128)(2,1)S(1)} %get-tuple-element.115), channel_id=1, source_target_pairs={{0,96},{1,97},{2,98},{3,99},{4,100},{5,101},{6,102},{7,103},{8,104... | collective-permute-start | bytes 884744 | tf_op jit(solution)/shard_map/ppermute | solution.py:888
  62.7 5.0 %collective-permute-done.21.rest_2_ = bf16[56,16,384]{2,1,0:T(8,128)(2,1)S(1)} collective-permute-done((bf16[56,16,384]{2,1,0:T(8,128)(2,1)S(1)}, bf16[56,16,384]{2,1,0:T(8,128)(2,1)S(1)}, u32[]{:S(2)}, u32[]{:S(2)}) %collective-permute-start.21) | collective-permute-done | bytes 688160 | tf_op jit(solution)/shard_map/ppermute | solution.py:888
  68.7 1.8 %collective-permute-start.23 = (bf16[224,384]{1,0:T(8,128)(2,1)S(1)}, bf16[224,384]{1,0:T(8,128)(2,1)S(1)}, u32[]{:S(2)}, u32[]{:S(2)}) collective-permute-start(bf16[224,384]{1,0:T(8,128)(2,1)S(1)} %get-tuple-element.125), channel_id=1, source_target_pairs={{0,64},{1,65},{2,66},{3,67},{4,68},{5,69},{6,70},{7,71},{8,72},{9,... | collective-permute-start | bytes 516104 | tf_op jit(solution)/shard_map/ppermute | solution.py:888
  70.4 1.4 %collective-permute-start.24 = (bf16[224,384]{1,0:T(8,128)(2,1)S(1)}, bf16[224,384]{1,0:T(8,128)(2,1)S(1)}, u32[]{:S(2)}, u32[]{:S(2)}) collective-permute-start(bf16[224,384]{1,0:T(8,128)(2,1)S(1)} %get-tuple-element.126), channel_id=1, source_target_pairs={{0,32},{1,33},{2,34},{3,35},{4,36},{5,37},{6,38},{7,39},{8,40},{9,... | collective-permute-start | bytes 516104 | tf_op jit(solution)/shard_map/ppermute | solution.py:888
  71.9 1.8 %collective-permute-start.25 = (bf16[224,384]{1,0:T(8,128)(2,1)S(1)}, bf16[224,384]{1,0:T(8,128)(2,1)S(1)}, u32[]{:S(2)}, u32[]{:S(2)}) collective-permute-start(bf16[224,384]{1,0:T(8,128)(2,1)S(1)} %get-tuple-element.127), channel_id=1, source_target_pairs={{0,96},{1,97},{2,98},{3,99},{4,100},{5,101},{6,102},{7,103},{8,104... | collective-permute-start | bytes 516104 | tf_op jit(solution)/shard_map/ppermute | solution.py:888
  74.1 2.5 %collective-permute-start.17 = (bf16[96,384]{1,0:T(8,128)(2,1)S(1)}, bf16[96,384]{1,0:T(8,128)(2,1)S(1)}, u32[]{:S(2)}, u32[]{:S(2)}) collective-permute-start(bf16[96,384]{1,0:T(8,128)(2,1)S(1)} %get-tuple-element.117), channel_id=1, source_target_pairs={{0,16},{1,5},{2,18},{3,7},{4,20},{5,1},{6,22},{7,3},{8,24},{9,13},... | collective-permute-start | bytes 221192 | tf_op jit(solution)/shard_map/ppermute | solution.py:888
  77.5 2.3 %collective-permute-start.19 = (bf16[96,384]{1,0:T(8,128)(2,1)S(1)}, bf16[96,384]{1,0:T(8,128)(2,1)S(1)}, u32[]{:S(2)}, u32[]{:S(2)}) collective-permute-start(bf16[96,384]{1,0:T(8,128)(2,1)S(1)} %get-tuple-element.119), channel_id=1, source_target_pairs={{0,24},{1,7},{2,26},{3,1},{4,28},{5,3},{6,30},{7,5},{8,0},{9,15},{... | collective-permute-start | bytes 221192 | tf_op jit(solution)/shard_map/ppermute | solution.py:888
  80.2 2.0 %collective-permute-done.18.rest_2_ = bf16[96,384]{1,0:T(8,128)(2,1)S(1)} collective-permute-done((bf16[96,384]{1,0:T(8,128)(2,1)S(1)}, bf16[96,384]{1,0:T(8,128)(2,1)S(1)}, u32[]{:S(2)}, u32[]{:S(2)}) %collective-permute-start.18) | collective-permute-done | bytes 73760 | tf_op jit(solution)/shard_map/ppermute | solution.py:888
  82.3 2.0 %collective-permute-start.26 = (bf16[80,384]{1,0:T(8,128)(2,1)S(1)}, bf16[80,384]{1,0:T(8,128)(2,1)S(1)}, u32[]{:S(2)}, u32[]{:S(2)}) collective-permute-start(bf16[80,384]{1,0:T(8,128)(2,1)S(1)} %get-tuple-element.129), channel_id=1, source_target_pairs={{0,4},{1,17},{2,6},{3,19},{4,0},{5,21},{6,2},{7,23},{8,12},{9,25},... | collective-permute-start | bytes 184328 | tf_op jit(solution)/shard_map/ppermute | solution.py:888
  84.3 1.9 %collective-permute-start.27 = (bf16[80,384]{1,0:T(8,128)(2,1)S(1)}, bf16[80,384]{1,0:T(8,128)(2,1)S(1)}, u32[]{:S(2)}, u32[]{:S(2)}) collective-permute-start(bf16[80,384]{1,0:T(8,128)(2,1)S(1)} %get-tuple-element.130), channel_id=1, source_target_pairs={{0,2},{1,9},{2,4},{3,11},{4,6},{5,13},{6,0},{7,15},{8,10},{9,17},{... | collective-permute-start | bytes 184328 | tf_op jit(solution)/shard_map/ppermute | solution.py:888
  86.2 1.3 %collective-permute-start.28 = (bf16[80,384]{1,0:T(8,128)(2,1)S(1)}, bf16[80,384]{1,0:T(8,128)(2,1)S(1)}, u32[]{:S(2)}, u32[]{:S(2)}) collective-permute-start(bf16[80,384]{1,0:T(8,128)(2,1)S(1)} %get-tuple-element.131), channel_id=1, source_target_pairs={{0,6},{1,25},{2,0},{3,27},{4,2},{5,29},{6,4},{7,31},{8,14},{9,1},{... | collective-permute-start | bytes 184328 | tf_op jit(solution)/shard_map/ppermute | solution.py:888
  88.1 1.7 %collective-permute-done.27.rest_2_ = bf16[80,384]{1,0:T(8,128)(2,1)S(1)} collective-permute-done((bf16[80,384]{1,0:T(8,128)(2,1)S(1)}, bf16[80,384]{1,0:T(8,128)(2,1)S(1)}, u32[]{:S(2)}, u32[]{:S(2)}) %collective-permute-start.27) | collective-permute-done | bytes 61472 | tf_op jit(solution)/shard_map/ppermute | solution.py:888
  (48 shorter events, 9.4 us)
Async XLA Ops:
  0.6 1.4 %collective-permute-start = (bf16[2,384]{1,0:T(2,128)(2,1)}, bf16[2,384]{1,0:T(2,128)(2,1)S(1)}, u32[]{:S(2)}, u32[]{:S(2)}) collective-permute-start(bf16[2,384]{1,0:T(2,128)(2,1)} %source.1), channel_id=1, source_target_pairs={{0,1},{1,0},{2,3},{3,2},{4,5},{5,4},{6,7},{7,6},{8,9},{9,8},{10,11... | collective-permute-start | bytes 4616 | tf_op jit(solution)/shard_map/ppermute | solution.py:892
  2.1 10.1 %collective-permute-start.3 = (bf16[2,2,384]{2,1,0:T(2,128)(2,1)S(1)}, bf16[2,2,384]{2,1,0:T(2,128)(2,1)S(1)}, u32[]{:S(2)}, u32[]{:S(2)}) collective-permute-start(bf16[2,2,384]{2,1,0:T(2,128)(2,1)S(1)} %join_cores.1.rest_0_), channel_id=1, source_target_pairs={{0,96},{1,97},{2,98},{3,99},{4,100},{5,101},{6,102},{7,103},{8,104... | collective-permute-start | bytes 9224 | tf_op jit(solution)/shard_map/ppermute | solution.py:888
  6.2 6.0 %collective-permute-start.2 = (bf16[2,2,384]{2,1,0:T(2,128)(2,1)S(1)}, bf16[2,2,384]{2,1,0:T(2,128)(2,1)S(1)}, u32[]{:S(2)}, u32[]{:S(2)}) collective-permute-start(bf16[2,2,384]{2,1,0:T(2,128)(2,1)S(1)} %join_cores.1.rest_0_), channel_id=1, source_target_pairs={{0,32},{1,33},{2,34},{3,35},{4,36},{5,37},{6,38},{7,39},{8,40},{9,... | collective-permute-start | bytes 9224 | tf_op jit(solution)/shard_map/ppermute | solution.py:888
  6.2 6.0 %collective-permute-start.1 = (bf16[2,2,384]{2,1,0:T(2,128)(2,1)S(1)}, bf16[2,2,384]{2,1,0:T(2,128)(2,1)S(1)}, u32[]{:S(2)}, u32[]{:S(2)}) collective-permute-start(bf16[2,2,384]{2,1,0:T(2,128)(2,1)S(1)} %join_cores.1.rest_0_), channel_id=1, source_target_pairs={{0,64},{1,65},{2,66},{3,67},{4,68},{5,69},{6,70},{7,71},{8,72},{9,... | collective-permute-start | bytes 9224 | tf_op jit(solution)/shard_map/ppermute | solution.py:888
  12.2 9.0 %collective-permute-start.6 = (bf16[4,2,2,384]{3,2,1,0:T(2,128)(2,1)S(1)}, bf16[4,2,2,384]{3,2,1,0:T(2,128)(2,1)S(1)}, u32[]{:S(2)}, u32[]{:S(2)}) collective-permute-start(bf16[4,2,2,384]{3,2,1,0:T(2,128)(2,1)S(1)} %gather_ring.2._.rest_0_), channel_id=1, source_target_pairs={{0,24},{1,25},{2,26},{3,27},{4,28},{5,29},{6,30},{7,31},{8,0},{9,1... | collective-permute-start | bytes 36872 | tf_op jit(solution)/shard_map/ppermute | solution.py:888
  15.0 6.2 %collective-permute-start.5 = (bf16[4,2,2,384]{3,2,1,0:T(2,128)(2,1)S(1)}, bf16[4,2,2,384]{3,2,1,0:T(2,128)(2,1)S(1)}, u32[]{:S(2)}, u32[]{:S(2)}) collective-permute-start(bf16[4,2,2,384]{3,2,1,0:T(2,128)(2,1)S(1)} %gather_ring.2._.rest_0_), channel_id=1, source_target_pairs={{0,8},{1,9},{2,10},{3,11},{4,12},{5,13},{6,14},{7,15},{8,16},{9,17... | collective-permute-start | bytes 36872 | tf_op jit(solution)/shard_map/ppermute | solution.py:888
  15.0 6.2 %collective-permute-start.4 = (bf16[4,2,2,384]{3,2,1,0:T(2,128)(2,1)S(1)}, bf16[4,2,2,384]{3,2,1,0:T(2,128)(2,1)S(1)}, u32[]{:S(2)}, u32[]{:S(2)}) collective-permute-start(bf16[4,2,2,384]{3,2,1,0:T(2,128)(2,1)S(1)} %gather_ring.2._.rest_0_), channel_id=1, source_target_pairs={{0,16},{1,17},{2,18},{3,19},{4,20},{5,21},{6,22},{7,23},{8,24},{9,... | collective-permute-start | bytes 36872 | tf_op jit(solution)/shard_map/ppermute | solution.py:888
  17.3 9.2 %copy-start.1 = (s32[2]{0:T(128)S(1)}, s32[2]{0:T(128)}, u32[]{:S(2)}) copy-start(s32[2]{0:T(128)} %counts.5) | copy-start | bytes 28
  21.3 8.4 %collective-permute-start.9 = (bf16[4,4,2,2,384]{4,3,2,1,0:T(2,128)(2,1)S(1)}, bf16[4,4,2,2,384]{4,3,2,1,0:T(2,128)(2,1)S(1)}, u32[]{:S(2)}, u32[]{:S(2)}) collective-permute-start(bf16[4,4,2,2,384]{4,3,2,1,0:T(2,128)(2,1)S(1)} %gather_ring.3._.rest_0_), channel_id=1, source_target_pairs={{0,6},{1,7},{2,0},{3,1},{4,2},{5,3},{6,4},{7,5},{8,14},{9,15},{10,... | collective-permute-start | bytes 147464 | tf_op jit(solution)/shard_map/ppermute | solution.py:888
  24.4 5.8 %collective-permute-start.8 = (bf16[4,4,2,2,384]{4,3,2,1,0:T(2,128)(2,1)S(1)}, bf16[4,4,2,2,384]{4,3,2,1,0:T(2,128)(2,1)S(1)}, u32[]{:S(2)}, u32[]{:S(2)}) collective-permute-start(bf16[4,4,2,2,384]{4,3,2,1,0:T(2,128)(2,1)S(1)} %gather_ring.3._.rest_0_), channel_id=1, source_target_pairs={{0,2},{1,3},{2,4},{3,5},{4,6},{5,7},{6,0},{7,1},{8,10},{9,11},{10,... | collective-permute-start | bytes 147464 | tf_op jit(solution)/shard_map/ppermute | solution.py:888
  24.4 5.8 %collective-permute-start.7 = (bf16[4,4,2,2,384]{4,3,2,1,0:T(2,128)(2,1)S(1)}, bf16[4,4,2,2,384]{4,3,2,1,0:T(2,128)(2,1)S(1)}, u32[]{:S(2)}, u32[]{:S(2)}) collective-permute-start(bf16[4,4,2,2,384]{4,3,2,1,0:T(2,128)(2,1)S(1)} %gather_ring.3._.rest_0_), channel_id=1, source_target_pairs={{0,4},{1,5},{2,6},{3,7},{4,0},{5,1},{6,2},{7,3},{8,12},{9,13},{10,... | collective-permute-start | bytes 147464 | tf_op jit(solution)/shard_map/ppermute | solution.py:888
  26.6 3.6 %copy-start = (s32[256]{0:T(256)S(1)}, s32[256]{0:T(256)}, u32[]{:S(2)}) copy-start(s32[256]{0:T(256)} %slot_of.3) | copy-start | bytes 3076
  37.0 10.2 %collective-permute-start.10 = (bf16[4,36,16,384]{3,2,1,0:T(8,128)(2,1)S(1)}, bf16[4,36,16,384]{3,2,1,0:T(8,128)(2,1)S(1)}, u32[]{:S(2)}, u32[]{:S(2)}) collective-permute-start(bf16[4,36,16,384]{3,2,1,0:T(8,128)(2,1)S(1)} %get-tuple-element.92), channel_id=1, source_target_pairs={{0,1},{1,0},{2,3},{3,2},{4,5},{5,4},{6,7},{7,6},{8,9},{9,8},{10,11... | collective-permute-start | bytes 5308424 | tf_op jit(solution)/shard_map/ppermute | solution.py:892
  40.3 6.9 %collective-permute-start.11 = (bf16[4,27,16,384]{3,2,1,0:T(8,128)(2,1)S(1)}, bf16[4,27,16,384]{3,2,1,0:T(8,128)(2,1)S(1)}, u32[]{:S(2)}, u32[]{:S(2)}) collective-permute-start(bf16[4,27,16,384]{3,2,1,0:T(8,128)(2,1)S(1)} %get-tuple-element.98), channel_id=1, source_target_pairs={{0,1},{1,0},{2,3},{3,2},{4,5},{5,4},{6,7},{7,6},{8,9},{9,8},{10,11... | collective-permute-start | bytes 3981320 | tf_op jit(solution)/shard_map/ppermute | solution.py:892
  44.1 3.1 %collective-permute-start.12 = (bf16[4,11,16,384]{3,2,1,0:T(8,128)(2,1)S(1)}, bf16[4,11,16,384]{3,2,1,0:T(8,128)(2,1)S(1)}, u32[]{:S(2)}, u32[]{:S(2)}) collective-permute-start(bf16[4,11,16,384]{3,2,1,0:T(8,128)(2,1)S(1)} %get-tuple-element.107), channel_id=1, source_target_pairs={{0,1},{1,0},{2,3},{3,2},{4,5},{5,4},{6,7},{7,6},{8,9},{9,8},{10,11... | collective-permute-start | bytes 1622024 | tf_op jit(solution)/shard_map/ppermute | solution.py:892
  45.4 1.8 %collective-permute-start.13 = (bf16[4,6,16,384]{3,2,1,0:T(8,128)(2,1)S(1)}, bf16[4,6,16,384]{3,2,1,0:T(8,128)(2,1)S(1)}, u32[]{:S(2)}, u32[]{:S(2)}) collective-permute-start(bf16[4,6,16,384]{3,2,1,0:T(8,128)(2,1)S(1)} %get-tuple-element.111), channel_id=1, source_target_pairs={{0,1},{1,0},{2,3},{3,2},{4,5},{5,4},{6,7},{7,6},{8,9},{9,8},{10,11... | collective-permute-start | bytes 884744 | tf_op jit(solution)/shard_map/ppermute | solution.py:892
  47.8 12.6 %collective-permute-start.20 = (bf16[56,16,384]{2,1,0:T(8,128)(2,1)S(1)}, bf16[56,16,384]{2,1,0:T(8,128)(2,1)S(1)}, u32[]{:S(2)}, u32[]{:S(2)}) collective-permute-start(bf16[56,16,384]{2,1,0:T(8,128)(2,1)S(1)} %get-tuple-element.121), channel_id=1, source_target_pairs={{0,16},{1,5},{2,18},{3,7},{4,20},{5,1},{6,22},{7,3},{8,24},{9,13},... | collective-permute-start | bytes 2064392 | tf_op jit(solution)/shard_map/ppermute | solution.py:888
  49.2 18.5 %collective-permute-start.21 = (bf16[56,16,384]{2,1,0:T(8,128)(2,1)S(1)}, bf16[56,16,384]{2,1,0:T(8,128)(2,1)S(1)}, u32[]{:S(2)}, u32[]{:S(2)}) collective-permute-start(bf16[56,16,384]{2,1,0:T(8,128)(2,1)S(1)} %get-tuple-element.122), channel_id=1, source_target_pairs={{0,8},{1,3},{2,10},{3,5},{4,12},{5,7},{6,14},{7,1},{8,16},{9,11},{... | collective-permute-start | bytes 2064392 | tf_op jit(solution)/shard_map/ppermute | solution.py:888
  51.0 16.7 %collective-permute-start.22 = (bf16[56,16,384]{2,1,0:T(8,128)(2,1)S(1)}, bf16[56,16,384]{2,1,0:T(8,128)(2,1)S(1)}, u32[]{:S(2)}, u32[]{:S(2)}) collective-permute-start(bf16[56,16,384]{2,1,0:T(8,128)(2,1)S(1)} %get-tuple-element.123), channel_id=1, source_target_pairs={{0,24},{1,7},{2,26},{3,1},{4,28},{5,3},{6,30},{7,5},{8,0},{9,15},{... | collective-permute-start | bytes 2064392 | tf_op jit(solution)/shard_map/ppermute | solution.py:888
  52.4 19.5 %collective-permute-start.14 = (bf16[24,16,384]{2,1,0:T(8,128)(2,1)S(1)}, bf16[24,16,384]{2,1,0:T(8,128)(2,1)S(1)}, u32[]{:S(2)}, u32[]{:S(2)}) collective-permute-start(bf16[24,16,384]{2,1,0:T(8,128)(2,1)S(1)} %get-tuple-element.113), channel_id=1, source_target_pairs={{0,64},{1,65},{2,66},{3,67},{4,68},{5,69},{6,70},{7,71},{8,72},{9,... | collective-permute-start | bytes 884744 | tf_op jit(solution)/shard_map/ppermute | solution.py:888
  54.1 19.6 %collective-permute-start.15 = (bf16[24,16,384]{2,1,0:T(8,128)(2,1)S(1)}, bf16[24,16,384]{2,1,0:T(8,128)(2,1)S(1)}, u32[]{:S(2)}, u32[]{:S(2)}) collective-permute-start(bf16[24,16,384]{2,1,0:T(8,128)(2,1)S(1)} %get-tuple-element.114), channel_id=1, source_target_pairs={{0,32},{1,33},{2,34},{3,35},{4,36},{5,37},{6,38},{7,39},{8,40},{9,... | collective-permute-start | bytes 884744 | tf_op jit(solution)/shard_map/ppermute | solution.py:888
  60.4 13.3 %collective-permute-start.16 = (bf16[24,16,384]{2,1,0:T(8,128)(2,1)S(1)}, bf16[24,16,384]{2,1,0:T(8,128)(2,1)S(1)}, u32[]{:S(2)}, u32[]{:S(2)}) collective-permute-start(bf16[24,16,384]{2,1,0:T(8,128)(2,1)S(1)} %get-tuple-element.115), channel_id=1, source_target_pairs={{0,96},{1,97},{2,98},{3,99},{4,100},{5,101},{6,102},{7,103},{8,104... | collective-permute-start | bytes 884744 | tf_op jit(solution)/shard_map/ppermute | solution.py:888
  68.7 8.8 %collective-permute-start.23 = (bf16[224,384]{1,0:T(8,128)(2,1)S(1)}, bf16[224,384]{1,0:T(8,128)(2,1)S(1)}, u32[]{:S(2)}, u32[]{:S(2)}) collective-permute-start(bf16[224,384]{1,0:T(8,128)(2,1)S(1)} %get-tuple-element.125), channel_id=1, source_target_pairs={{0,64},{1,65},{2,66},{3,67},{4,68},{5,69},{6,70},{7,71},{8,72},{9,... | collective-permute-start | bytes 516104 | tf_op jit(solution)/shard_map/ppermute | solution.py:888
  70.4 9.7 %collective-permute-start.24 = (bf16[224,384]{1,0:T(8,128)(2,1)S(1)}, bf16[224,384]{1,0:T(8,128)(2,1)S(1)}, u32[]{:S(2)}, u32[]{:S(2)}) collective-permute-start(bf16[224,384]{1,0:T(8,128)(2,1)S(1)} %get-tuple-element.126), channel_id=1, source_target_pairs={{0,32},{1,33},{2,34},{3,35},{4,36},{5,37},{6,38},{7,39},{8,40},{9,... | collective-permute-start | bytes 516104 | tf_op jit(solution)/shard_map/ppermute | solution.py:888
  71.9 8.2 %collective-permute-start.25 = (bf16[224,384]{1,0:T(8,128)(2,1)S(1)}, bf16[224,384]{1,0:T(8,128)(2,1)S(1)}, u32[]{:S(2)}, u32[]{:S(2)}) collective-permute-start(bf16[224,384]{1,0:T(8,128)(2,1)S(1)} %get-tuple-element.127), channel_id=1, source_target_pairs={{0,96},{1,97},{2,98},{3,99},{4,100},{5,101},{6,102},{7,103},{8,104... | collective-permute-start | bytes 516104 | tf_op jit(solution)/shard_map/ppermute | solution.py:888
  74.1 6.1 %collective-permute-start.17 = (bf16[96,384]{1,0:T(8,128)(2,1)S(1)}, bf16[96,384]{1,0:T(8,128)(2,1)S(1)}, u32[]{:S(2)}, u32[]{:S(2)}) collective-permute-start(bf16[96,384]{1,0:T(8,128)(2,1)S(1)} %get-tuple-element.117), channel_id=1, source_target_pairs={{0,16},{1,5},{2,18},{3,7},{4,20},{5,1},{6,22},{7,3},{8,24},{9,13},... | collective-permute-start | bytes 221192 | tf_op jit(solution)/shard_map/ppermute | solution.py:888
  76.6 5.6 %collective-permute-start.18 = (bf16[96,384]{1,0:T(8,128)(2,1)S(1)}, bf16[96,384]{1,0:T(8,128)(2,1)S(1)}, u32[]{:S(2)}, u32[]{:S(2)}) collective-permute-start(bf16[96,384]{1,0:T(8,128)(2,1)S(1)} %get-tuple-element.118), channel_id=1, source_target_pairs={{0,8},{1,3},{2,10},{3,5},{4,12},{5,7},{6,14},{7,1},{8,16},{9,11},{... | collective-permute-start | bytes 221192 | tf_op jit(solution)/shard_map/ppermute | solution.py:888
  77.5 4.7 %collective-permute-start.19 = (bf16[96,384]{1,0:T(8,128)(2,1)S(1)}, bf16[96,384]{1,0:T(8,128)(2,1)S(1)}, u32[]{:S(2)}, u32[]{:S(2)}) collective-permute-start(bf16[96,384]{1,0:T(8,128)(2,1)S(1)} %get-tuple-element.119), channel_id=1, source_target_pairs={{0,24},{1,7},{2,26},{3,1},{4,28},{5,3},{6,30},{7,5},{8,0},{9,15},{... | collective-permute-start | bytes 221192 | tf_op jit(solution)/shard_map/ppermute | solution.py:888
  82.3 5.8 %collective-permute-start.26 = (bf16[80,384]{1,0:T(8,128)(2,1)S(1)}, bf16[80,384]{1,0:T(8,128)(2,1)S(1)}, u32[]{:S(2)}, u32[]{:S(2)}) collective-permute-start(bf16[80,384]{1,0:T(8,128)(2,1)S(1)} %get-tuple-element.129), channel_id=1, source_target_pairs={{0,4},{1,17},{2,6},{3,19},{4,0},{5,21},{6,2},{7,23},{8,12},{9,25},... | collective-permute-start | bytes 184328 | tf_op jit(solution)/shard_map/ppermute | solution.py:888
  84.3 5.4 %collective-permute-start.27 = (bf16[80,384]{1,0:T(8,128)(2,1)S(1)}, bf16[80,384]{1,0:T(8,128)(2,1)S(1)}, u32[]{:S(2)}, u32[]{:S(2)}) collective-permute-start(bf16[80,384]{1,0:T(8,128)(2,1)S(1)} %get-tuple-element.130), channel_id=1, source_target_pairs={{0,2},{1,9},{2,4},{3,11},{4,6},{5,13},{6,0},{7,15},{8,10},{9,17},{... | collective-permute-start | bytes 184328 | tf_op jit(solution)/shard_map/ppermute | solution.py:888
  86.2 4.2 %collective-permute-start.28 = (bf16[80,384]{1,0:T(8,128)(2,1)S(1)}, bf16[80,384]{1,0:T(8,128)(2,1)S(1)}, u32[]{:S(2)}, u32[]{:S(2)}) collective-permute-start(bf16[80,384]{1,0:T(8,128)(2,1)S(1)} %get-tuple-element.131), channel_id=1, source_target_pairs={{0,6},{1,25},{2,0},{3,27},{4,2},{5,29},{6,4},{7,31},{8,14},{9,1},{... | collective-permute-start | bytes 184328 | tf_op jit(solution)/shard_map/ppermute | solution.py:888
